TPU v7x, 512 devices: a whole 4x4x16 slice. The times are simulated.
512 devices in a mesh: stream: 16 (over z_lo, y), cross: 32 (over z_hi, x, core).
Axes of the slice: x: 4, y: 4, z: 16 (z_hi: 4, z_lo: 4; z = z_hi * 4 + z_lo), core: 2. Of those that a mesh axis runs over, the one named last changes fastest.
Arguments:
- vof: bfloat16 [6144, 512], P(('stream', 'cross')), may hold values from 0 to 1
- target: bfloat16 [6144, 512], P(('stream', 'cross')), may hold values from -21 to 21
- neighbours: int32 [6144, 26], P(('stream', 'cross')), may hold values from -1 to 6143, as said below
- live_blocks: int32 [512], P(('stream', 'cross')), may hold values from 2 to 12, as said below
- pick: int32 [512, 2], P(('stream', 'cross')), may hold values from -1 to 191, as said below
- w_first: bfloat16 [125, 128], replicated, may hold values from -0.5 to 0.5
- w_mid: bfloat16 [2, 128, 128], replicated, may hold values from -0.5 to 0.5
- w_last: bfloat16 [128], replicated, may hold values from -0.5 to 0.5
Outputs:
- prediction: float32 [4096, 512], P(('stream', 'cross'))
- grad_first: float32 [125, 128], replicated
- grad_mid: float32 [2, 128, 128], replicated
- grad_last: float32 [128], replicated
Inputs may be any that keep to these rules, and one draw needn't show every extreme that they name: Home slots 0 to live_blocks[d] - 1 of device d hold interface blocks and the rest are empty; in every slab 8 devices hold more than 6 blocks and the others at most 6. `neighbours`: an entry names a live home slot of a device whose stream index and cross index each differ from those of the block's own device by at most one. `pick`: in each slab every live home slot 6 + j of the device with cross index c is named, as c * 6 + j, by exactly one entry of one device of that slab; devices holding more than 6 blocks name none.
All inputs are finite; a program needn't handle non-finite values.
Results may differ from a plain program's by a relative error of at most 0.003.
The roundings to bfloat16 on the way count: a program that leaves them out, or rounds other values in their place, can miss the bound.
Values may be sent and summed in bfloat16 or wider, within the bound.
A program may use at most 128 MiB of HBM per device.

v0:
```python
import jax
import jax.numpy as jnp
from jax import lax
from jax.sharding import PartitionSpec as P

FEAT = 125
BE = 8
KEEP = 6
RECV = 2
PADROW = 1792


def from_behind(block, axis, distance):
    devices = range(lax.axis_size(axis))
    route = [(i - distance, i) for i in devices if i - distance in devices]
    return lax.ppermute(block, axis, route)


def assemble(center, border, block_edge):
    number = center.shape[0]
    pieces = jnp.concatenate([border[:, :13], center[:, None], border[:, 13:]], axis=1)
    shaped = pieces.reshape(number, 3, 3, 3, block_edge, block_edge, block_edge)
    shaped = shaped.transpose(0, 1, 4, 2, 5, 3, 6).reshape(
        number, 3 * block_edge, 3 * block_edge, 3 * block_edge
    )
    lower = block_edge - 2
    upper = 2 * block_edge + 2
    return shaped[:, lower:upper, lower:upper, lower:upper]


def stencil(padded, block_edge):
    columns = []
    for along_x in range(5):
        for along_y in range(5):
            for along_z in range(5):
                window = padded[
                    :,
                    along_x : along_x + block_edge,
                    along_y : along_y + block_edge,
                    along_z : along_z + block_edge,
                ]
                columns.append(window.reshape(-1))
    return jnp.stack(columns)


def contract_rows(former, latter):
    return lax.dot_general(
        former, latter, (((0,), (0,)), ((), ())), preferred_element_type=jnp.float32
    )


def contract_cols(former, latter):
    return lax.dot_general(
        former, latter, (((1,), (1,)), ((), ())), preferred_element_type=jnp.float32
    )


def train_terms(features, target_row, weight_mask, w_first, w_mid, w_last, loss_scale):
    hidden_one = jnp.tanh(contract_rows(w_first, features)).astype(jnp.bfloat16)
    hidden_two = jnp.tanh(contract_rows(w_mid[0], hidden_one)).astype(jnp.bfloat16)
    hidden_three = jnp.tanh(contract_rows(w_mid[1], hidden_two)).astype(jnp.bfloat16)
    predicted = jnp.dot(w_last, hidden_three, preferred_element_type=jnp.float32) * weight_mask
    residual = ((predicted - target_row.astype(jnp.float32)) * weight_mask / loss_scale).astype(
        jnp.bfloat16
    )
    grad_last = jnp.dot(hidden_three, residual, preferred_element_type=jnp.float32)
    slope_three = 1.0 - jnp.square(hidden_three.astype(jnp.float32))
    delta_three = (
        w_last.astype(jnp.float32)[:, None] * residual.astype(jnp.float32)[None, :] * slope_three
    ).astype(jnp.bfloat16)
    grad_third = contract_cols(hidden_two, delta_three)
    slope_two = 1.0 - jnp.square(hidden_two.astype(jnp.float32))
    delta_two = (
        jnp.dot(w_mid[1], delta_three, preferred_element_type=jnp.float32) * slope_two
    ).astype(jnp.bfloat16)
    grad_second = contract_cols(hidden_one, delta_two)
    slope_one = 1.0 - jnp.square(hidden_one.astype(jnp.float32))
    delta_one = (
        jnp.dot(w_mid[0], delta_two, preferred_element_type=jnp.float32) * slope_one
    ).astype(jnp.bfloat16)
    grad_first = contract_cols(features, delta_one)
    return (predicted, grad_first, jnp.stack([grad_second, grad_third]), grad_last)


def shards(vof, target, neighbours, live_blocks, pick, w_first, w_mid, w_last):
    home_blocks = vof.shape[0]
    cell_count = vof.shape[1]
    cross_size = lax.axis_size("cross")
    stream_size = lax.axis_size("stream")
    slab_index = lax.axis_index("stream")
    cross_index = lax.axis_index("cross")
    below = from_behind(vof, "stream", 1)
    above = from_behind(vof, "stream", -1)
    column = jnp.stack([below, vof, above])
    left = from_behind(column, "cross", 1)
    right = from_behind(column, "cross", -1)
    beside_all = jnp.stack([left, column, right], axis=1)
    table = jnp.concatenate(
        [beside_all.reshape(9 * home_blocks, cell_count), jnp.zeros((1, cell_count), vof.dtype)],
        axis=0,
    )
    owner_device = neighbours // home_blocks
    slab_step = owner_device // cross_size - slab_index + 1
    cross_step = owner_device % cross_size - cross_index + 1
    lookup = (slab_step * 3 + cross_step) * home_blocks + neighbours % home_blocks
    lookup = jnp.where(neighbours < 0, 9 * home_blocks, lookup)
    border = jnp.take(table, lookup, axis=0)
    padded = assemble(vof, border, BE)
    live_count = live_blocks[0]
    home_mask = (jnp.arange(home_blocks) < live_count).astype(jnp.float32)
    loss_scale = float(cell_count * KEEP * cross_size * stream_size)
    chosen = pick[0]
    padded_edge = padded.shape[1]
    flat_rows = padded.reshape(home_blocks, padded_edge**3)
    flat_rows = jnp.pad(flat_rows, ((0, 0), (0, PADROW - padded_edge**3)))
    pieces = (
        lax.all_gather(flat_rows[KEEP:], "cross", axis=0, tiled=True),
        lax.all_gather(target[KEEP:], "cross", axis=0, tiled=True),
    )
    selector = (chosen[:, None] == jnp.arange(pieces[0].shape[0])[None, :]).astype(jnp.bfloat16)
    got_blocks = jnp.dot(selector, pieces[0], preferred_element_type=jnp.float32)
    got_targets = jnp.dot(selector, pieces[1], preferred_element_type=jnp.float32)
    got_blocks = got_blocks.astype(jnp.bfloat16)
    got_targets = got_targets.astype(jnp.bfloat16)
    got_blocks = got_blocks[:, : padded_edge**3].reshape(
        RECV, padded_edge, padded_edge, padded_edge
    )
    work_padded = jnp.concatenate([padded[:KEEP], got_blocks], axis=0)
    work_target = jnp.concatenate([target[:KEEP], got_targets], axis=0)
    block_mask = jnp.concatenate([home_mask[:KEEP], (chosen >= 0).astype(jnp.float32)])
    predicted, grad_first, grad_mid, grad_last = train_terms(
        stencil(work_padded, BE),
        work_target.reshape(-1),
        jnp.repeat(block_mask, cell_count),
        w_first,
        w_mid,
        w_last,
        loss_scale,
    )
    prediction = predicted.reshape(KEEP + RECV, cell_count)
    hidden_size = grad_last.shape[0]
    packed = jnp.concatenate(
        [
            grad_first,
            grad_last[None, :],
            jnp.zeros((128 - FEAT - 1, hidden_size), jnp.float32),
            grad_mid.reshape(2 * hidden_size, hidden_size),
        ],
        axis=0,
    )
    summed = lax.psum(packed, ("stream", "cross"))
    return (
        prediction,
        summed[:FEAT],
        summed[128:].reshape(2, hidden_size, hidden_size),
        summed[FEAT],
    )


def solution(mesh):
    return jax.shard_map(
        shards,
        mesh=mesh,
        in_specs=(
            P(("stream", "cross"), None),
            P(("stream", "cross"), None),
            P(("stream", "cross"), None),
            P(("stream", "cross")),
            P(("stream", "cross"), None),
            P(),
            P(),
            P(),
        ),
        out_specs=(P(("stream", "cross"), None), P(), P(), P()),
        check_vma=False,
    )
```

profile of v0, /device:TPU:1, one launch (start us, length us, event | category | flops | bytes accessed | tf_op | source)
XLA Modules:
  0.0 796.8 jit_solution(742776914680141394)
XLA Ops:
  7.2 4.0 collective-permute-start
  11.3 1.3 collective-permute-start.1
  13.4 60.5 %all-gather.1 = bf16[32,6,512]{2,1,0:T(8,128)(2,1)S(1)} all-gather(bf16[1,6,512]{2,1,0:T(8,128)(2,1)S(1)} %get-tuple-element.139), channel_id=1, replica_groups=mesh['stream'=16,'cross'=32] {'cross'}, dimensions={0}, use_global_device_ids=true | all-gather | bytes 202752 | tf_op jit(solution)/shard_map/all_gather | solution.py:118
  77.8 1.9 collective-permute-start.2
  79.7 2.4 collective-permute-start.3
  86.1 2.0 gather_fusion
  88.6 7.5 reshape.47
  96.0 12.7 %copy.151 = bf16[12,3,8,3,8,3,8]{0,6,5,4,3,2,1:T(8,128)(2,1)} copy(bf16[12,3,8,3,8,3,8]{6,4,2,5,3,1,0:T(8,128)(2,1)} %bitcast.318) | data formatting | bytes 663552 | tf_op jit(solution)/shard_map/transpose | solution.py:23
  108.7 1.4 slice.565
  110.2 1.4 slice.564
  112.1 53.0 %all-gather = bf16[32,6,1792]{2,1,0:T(8,128)(2,1)S(1)} all-gather(bf16[1,6,1792]{2,1,0:T(8,128)(2,1)S(1)} %fusion.18), channel_id=1, replica_groups=mesh['stream'=16,'cross'=32] {'cross'}, dimensions={0}, use_global_device_ids=true | all-gather | bytes 709632 | tf_op jit(solution)/shard_map/all_gather | solution.py:117
  169.6 1.2 slice_maximum_fusion.14
  170.8 1.3 slice_maximum_fusion.15
  172.1 1.2 slice_maximum_fusion.16
  175.7 1.3 slice_maximum_fusion.19
  176.9 1.3 slice_maximum_fusion.20
  178.2 1.3 slice_maximum_fusion.21
  179.4 1.3 slice_maximum_fusion.22
  181.8 1.3 slice_maximum_fusion.24
  183.1 1.3 slice_maximum_fusion.25
  184.4 1.3 slice_maximum_fusion.26
  185.6 1.3 slice_maximum_fusion.27
  190.4 1.3 slice_maximum_fusion.10
  194.0 1.4 slice_maximum_fusion.7
  196.6 1.3 slice_maximum_fusion.5
  310.7 9.6 %stack.44 = bf16[125,4096]{1,0:T(8,128)(2,1)S(1)} concatenate(bf16[1,4096]{1,0:T(2,128)(2,1)S(1)} %stack_reshape.375, bf16[1,4096]{1,0:T(2,128)(2,1)S(1)} %stack_reshape.376, bf16[1,4096]{1,0:T(2,128)(2,1)S(1)} %stack_reshape.377, bf16[1,4096]{1,0:T(2,128)(2,1)S(1)} %stack_reshape.378, bf16[1,4096]{1,0:T(2,128)(2,1)S(1)} %stack_reshape.379, bf16[1,4096]{1,0:T(2,128)(2,1)S(1)} %stack_reshape.380, ...), dimensions={0} | concatenate | bytes 2048000 | tf_op jit(solution)/shard_map/stack | solution.py:43
  322.2 1.8 fusion.3
  324.0 2.1 fusion.6
  326.1 1.8 convolution_bitcast_fusion.1
  330.7 454.9 %all-reduce.4.cloned.1.call-done = f32[384,128]{1,0:T(8,128)} async-done(((f32[384,128]{1,0:T(8,128)}), f32[384,128]{1,0:T(8,128)}) %all-reduce.4.cloned.1.call-update) | async-done | bytes 196624 | tf_op jit(solution)/shard_map/psum | solution.py:151
  785.5 1.6 slice.816
  787.1 1.5 slice.815
  (626 shorter events, 140.0 us)
Async XLA Ops:
  7.2 313.1 %copy-start = (bf16[125,128]{1,0:T(8,128)(2,1)S(1)}, bf16[125,128]{1,0:T(8,128)(2,1)}, u32[]{:S(2)}) copy-start(bf16[125,128]{1,0:T(8,128)(2,1)} %param.13) | copy-start | bytes 96004
  7.2 778.4 %all-reduce.4.cloned.1.call-start = ((), (), s32[]{:S(2)}) async-start(), calls=%async_computation | async-start | bytes 393216 | tf_op jit(solution)/shard_map/psum | solution.py:151
  7.2 69.8 %collective-permute-start = (bf16[12,512]{1,0:T(8,128)(2,1)}, bf16[12,512]{1,0:T(8,128)(2,1)S(1)}, u32[]{:S(2)}, u32[]{:S(2)}) collective-permute-start(bf16[12,512]{1,0:T(8,128)(2,1)} %param.8), channel_id=1, source_target_pairs={{0,32},{32,64},{64,96},{96,128},{128,160},{160,192},{192,224},{224... | collective-permute-start | bytes 36872 | tf_op jit(solution)/shard_map/ppermute | solution.py:16
  11.3 65.8 %collective-permute-start.1 = (bf16[12,512]{1,0:T(8,128)(2,1)}, bf16[12,512]{1,0:T(8,128)(2,1)S(1)}, u32[]{:S(2)}, u32[]{:S(2)}) collective-permute-start(bf16[12,512]{1,0:T(8,128)(2,1)} %param.8), channel_id=1, source_target_pairs={{32,0},{64,32},{96,64},{128,96},{160,128},{192,160},{224,192},{256... | collective-permute-start | bytes 36872 | tf_op jit(solution)/shard_map/ppermute | solution.py:16
  77.8 8.2 %collective-permute-start.2 = (bf16[3,12,512]{2,1,0:T(8,128)(2,1)S(1)}, bf16[3,12,512]{2,1,0:T(8,128)(2,1)S(1)}, u32[]{:S(2)}, u32[]{:S(2)}) collective-permute-start(bf16[3,12,512]{2,1,0:T(8,128)(2,1)S(1)} %get-tuple-element.137), channel_id=1, source_target_pairs={{0,1},{1,2},{2,3},{3,4},{4,5},{5,6},{6,7},{7,8},{8,9},{9,10},{10,1... | collective-permute-start | bytes 110600 | tf_op jit(solution)/shard_map/ppermute | solution.py:16
  79.7 6.2 collective-permute-start.3
  111.6 53.7 %copy-start.151 = (s32[1,2]{1,0:T(1,128)S(1)}, s32[1,2]{1,0:T(1,128)}, u32[]{:S(2)}) copy-start(s32[1,2]{1,0:T(1,128)} %param.12) | copy-start | bytes 28
  204.8 11.7 %copy-start.97 = (bf16[8,8,8,8]{0,3,2,1:T(8,128)(2,1)S(1)}, bf16[8,8,8,8]{0,3,2,1:T(8,128)(2,1)}, u32[]{:S(2)}) copy-start(bf16[8,8,8,8]{0,3,2,1:T(8,128)(2,1)} %get-tuple-element.79) | copy-start | bytes 24580
  205.2 12.3 %copy-start.96 = (bf16[8,8,8,8]{0,3,2,1:T(8,128)(2,1)S(1)}, bf16[8,8,8,8]{0,3,2,1:T(8,128)(2,1)}, u32[]{:S(2)}) copy-start(bf16[8,8,8,8]{0,3,2,1:T(8,128)(2,1)} %get-tuple-element.80) | copy-start | bytes 24580
  206.3 12.3 %copy-start.95 = (bf16[8,8,8,8]{0,3,2,1:T(8,128)(2,1)S(1)}, bf16[8,8,8,8]{0,3,2,1:T(8,128)(2,1)}, u32[]{:S(2)}) copy-start(bf16[8,8,8,8]{0,3,2,1:T(8,128)(2,1)} %get-tuple-element.81) | copy-start | bytes 24580
  207.4 12.3 %copy-start.94 = (bf16[8,8,8,8]{0,3,2,1:T(8,128)(2,1)S(1)}, bf16[8,8,8,8]{0,3,2,1:T(8,128)(2,1)}, u32[]{:S(2)}) copy-start(bf16[8,8,8,8]{0,3,2,1:T(8,128)(2,1)} %get-tuple-element.83) | copy-start | bytes 24580
  208.4 12.3 %copy-start.93 = (bf16[8,8,8,8]{0,3,2,1:T(8,128)(2,1)S(1)}, bf16[8,8,8,8]{0,3,2,1:T(8,128)(2,1)}, u32[]{:S(2)}) copy-start(bf16[8,8,8,8]{0,3,2,1:T(8,128)(2,1)} %get-tuple-element.84) | copy-start | bytes 24580
  213.6 11.7 %copy-start.89 = (bf16[8,8,8,8]{0,3,2,1:T(8,128)(2,1)S(1)}, bf16[8,8,8,8]{0,3,2,1:T(8,128)(2,1)}, u32[]{:S(2)}) copy-start(bf16[8,8,8,8]{0,3,2,1:T(8,128)(2,1)} %get-tuple-element.89) | copy-start | bytes 24580
  214.7 11.7 %copy-start.88 = (bf16[8,8,8,8]{0,3,2,1:T(8,128)(2,1)S(1)}, bf16[8,8,8,8]{0,3,2,1:T(8,128)(2,1)}, u32[]{:S(2)}) copy-start(bf16[8,8,8,8]{0,3,2,1:T(8,128)(2,1)} %get-tuple-element.91) | copy-start | bytes 24580
  215.7 11.7 %copy-start.87 = (bf16[8,8,8,8]{0,3,2,1:T(8,128)(2,1)S(1)}, bf16[8,8,8,8]{0,3,2,1:T(8,128)(2,1)}, u32[]{:S(2)}) copy-start(bf16[8,8,8,8]{0,3,2,1:T(8,128)(2,1)} %get-tuple-element.92) | copy-start | bytes 24580
  216.8 11.7 %copy-start.86 = (bf16[8,8,8,8]{0,3,2,1:T(8,128)(2,1)S(1)}, bf16[8,8,8,8]{0,3,2,1:T(8,128)(2,1)}, u32[]{:S(2)}) copy-start(bf16[8,8,8,8]{0,3,2,1:T(8,128)(2,1)} %get-tuple-element.93) | copy-start | bytes 24580
  217.9 11.7 %copy-start.85 = (bf16[8,8,8,8]{0,3,2,1:T(8,128)(2,1)S(1)}, bf16[8,8,8,8]{0,3,2,1:T(8,128)(2,1)}, u32[]{:S(2)}) copy-start(bf16[8,8,8,8]{0,3,2,1:T(8,128)(2,1)} %get-tuple-element.95) | copy-start | bytes 24580
  218.9 11.6 %copy-start.84 = (bf16[8,8,8,8]{0,3,2,1:T(8,128)(2,1)S(1)}, bf16[8,8,8,8]{0,3,2,1:T(8,128)(2,1)}, u32[]{:S(2)}) copy-start(bf16[8,8,8,8]{0,3,2,1:T(8,128)(2,1)} %get-tuple-element.96) | copy-start | bytes 24580
  220.0 11.6 %copy-start.83 = (bf16[8,8,8,8]{0,3,2,1:T(8,128)(2,1)S(1)}, bf16[8,8,8,8]{0,3,2,1:T(8,128)(2,1)}, u32[]{:S(2)}) copy-start(bf16[8,8,8,8]{0,3,2,1:T(8,128)(2,1)} %get-tuple-element.97) | copy-start | bytes 24580
  222.1 11.7 %copy-start.81 = (bf16[8,8,8,8]{0,3,2,1:T(8,128)(2,1)S(1)}, bf16[8,8,8,8]{0,3,2,1:T(8,128)(2,1)}, u32[]{:S(2)}) copy-start(bf16[8,8,8,8]{0,3,2,1:T(8,128)(2,1)} %get-tuple-element.100) | copy-start | bytes 24580
  250.1 11.8 %copy-start.55 = (bf16[8,8,8,8]{0,3,2,1:T(8,128)(2,1)S(1)}, bf16[8,8,8,8]{0,3,2,1:T(8,128)(2,1)}, u32[]{:S(2)}) copy-start(bf16[8,8,8,8]{0,3,2,1:T(8,128)(2,1)} %get-tuple-element.130) | copy-start | bytes 24580
  251.2 11.8 %copy-start.54 = (bf16[8,8,8,8]{0,3,2,1:T(8,128)(2,1)S(1)}, bf16[8,8,8,8]{0,3,2,1:T(8,128)(2,1)}, u32[]{:S(2)}) copy-start(bf16[8,8,8,8]{0,3,2,1:T(8,128)(2,1)} %get-tuple-element.126) | copy-start | bytes 24580
  252.2 11.8 %copy-start.53 = (bf16[8,8,8,8]{0,3,2,1:T(8,128)(2,1)S(1)}, bf16[8,8,8,8]{0,3,2,1:T(8,128)(2,1)}, u32[]{:S(2)}) copy-start(bf16[8,8,8,8]{0,3,2,1:T(8,128)(2,1)} %get-tuple-element.122) | copy-start | bytes 24580
  253.3 11.8 %copy-start.52 = (bf16[8,8,8,8]{0,3,2,1:T(8,128)(2,1)S(1)}, bf16[8,8,8,8]{0,3,2,1:T(8,128)(2,1)}, u32[]{:S(2)}) copy-start(bf16[8,8,8,8]{0,3,2,1:T(8,128)(2,1)} %get-tuple-element.118) | copy-start | bytes 24580
  254.4 11.8 %copy-start.51 = (bf16[8,8,8,8]{0,3,2,1:T(8,128)(2,1)S(1)}, bf16[8,8,8,8]{0,3,2,1:T(8,128)(2,1)}, u32[]{:S(2)}) copy-start(bf16[8,8,8,8]{0,3,2,1:T(8,128)(2,1)} %get-tuple-element.114) | copy-start | bytes 24580
  255.4 11.8 %copy-start.50 = (bf16[8,8,8,8]{0,3,2,1:T(8,128)(2,1)S(1)}, bf16[8,8,8,8]{0,3,2,1:T(8,128)(2,1)}, u32[]{:S(2)}) copy-start(bf16[8,8,8,8]{0,3,2,1:T(8,128)(2,1)} %get-tuple-element.110) | copy-start | bytes 24580
  256.5 11.8 %copy-start.49 = (bf16[8,8,8,8]{0,3,2,1:T(8,128)(2,1)S(1)}, bf16[8,8,8,8]{0,3,2,1:T(8,128)(2,1)}, u32[]{:S(2)}) copy-start(bf16[8,8,8,8]{0,3,2,1:T(8,128)(2,1)} %get-tuple-element.106) | copy-start | bytes 24580
  257.6 11.8 %copy-start.48 = (bf16[8,8,8,8]{0,3,2,1:T(8,128)(2,1)S(1)}, bf16[8,8,8,8]{0,3,2,1:T(8,128)(2,1)}, u32[]{:S(2)}) copy-start(bf16[8,8,8,8]{0,3,2,1:T(8,128)(2,1)} %get-tuple-element.102) | copy-start | bytes 24580
  258.6 11.8 %copy-start.47 = (bf16[8,8,8,8]{0,3,2,1:T(8,128)(2,1)S(1)}, bf16[8,8,8,8]{0,3,2,1:T(8,128)(2,1)}, u32[]{:S(2)}) copy-start(bf16[8,8,8,8]{0,3,2,1:T(8,128)(2,1)} %get-tuple-element.98) | copy-start | bytes 24580
  259.7 11.8 %copy-start.46 = (bf16[8,8,8,8]{0,3,2,1:T(8,128)(2,1)S(1)}, bf16[8,8,8,8]{0,3,2,1:T(8,128)(2,1)}, u32[]{:S(2)}) copy-start(bf16[8,8,8,8]{0,3,2,1:T(8,128)(2,1)} %get-tuple-element.94) | copy-start | bytes 24580
  270.8 12.4 %copy-start.45 = (bf16[8,8,8,8]{0,3,2,1:T(8,128)(2,1)S(1)}, bf16[8,8,8,8]{0,3,2,1:T(8,128)(2,1)}, u32[]{:S(2)}) copy-start(bf16[8,8,8,8]{0,3,2,1:T(8,128)(2,1)} %get-tuple-element.60) | copy-start | bytes 24580
  271.8 11.8 %copy-start.44 = (bf16[8,8,8,8]{0,3,2,1:T(8,128)(2,1)S(1)}, bf16[8,8,8,8]{0,3,2,1:T(8,128)(2,1)}, u32[]{:S(2)}) copy-start(bf16[8,8,8,8]{0,3,2,1:T(8,128)(2,1)} %get-tuple-element.61) | copy-start | bytes 24580
  (127 other events, 959.4 us)
Sparse Core Ops, SparseCore 0:
  330.2 455.2 all-reduce.3
where the time goes:
time: 803 us; the launch traced here: 797 us
  waiting for transfers between devices  455 us (57%)
  local copies, waits for them, and re-layouts  152 us (19%)
  blocking collectives  114 us (14%)
  other arithmetic  39.4 us (5%)
  between operations  17.8 us (2%)
  matrix products  9.76 us (1%)
  starting transfers between devices  9.69 us (1%)
    psum x1, waiting for transfers between devices, shards(): summed = lax.psum(packed, ('stream', 'cross'))  455 us
    another operation x126, local copies, waits for them, and re-layouts, stencil(): return jnp.stack(columns)  77.5 us
    all_gather x1, blocking collectives, shards(): lax.all_gather(target[KEEP:], 'cross', axis=0, tiled=True)  60.5 us
    all_gather x1, blocking collectives, shards(): lax.all_gather(flat_rows[KEEP:], 'cross', axis=0, tiled=True)  53 us
    slice x125, local copies, waits for them, and re-layouts, stencil(): padded[:, along_x:along_x + block_edge, along_y:along_y + block_edge, alo...  38.1 us
    concatenate x31, other arithmetic, shards(): work_padded = jnp.concatenate([padded[:KEEP], got_blocks], axis=0)  34.8 us
  transfers between devices with their start and end apart: 5, of which 1 were waited for; matrix products, arithmetic and copies ran while one was open for 1% of the time, Pallas kernels for 0%

commit v1 on v0

v1 whole, which is shorter than its diff:
```python
import jax
import jax.numpy as jnp
from jax import lax
from jax.experimental import pallas as pl
from jax.experimental.pallas import tpu as pltpu
from jax.sharding import PartitionSpec as P

MESH = pl.DeviceIdType.MESH
F32 = jnp.float32
BF16 = jnp.bfloat16

KEEP = 6
HOME = 12
ROWS = 768
WIN = 384
SCALE = 1572864.0
SLABS = 16
CROSS = 32
PIECE = 12
PLANE = 32
VMEM = pl.BlockSpec(memory_space=pltpu.VMEM)
SMEM = pl.BlockSpec(memory_space=pltpu.SMEM)


def lanes(shape):
    return lax.broadcasted_iota(jnp.int32, shape, len(shape) - 1)


def shift(x, by):
    by = by % 128
    return x if by == 0 else pltpu.roll(x, by, x.ndim - 1)


def spread(rows, store, stride, first):
    lane = lanes(rows[:, :128].shape)
    for y in range(8):
        total = jnp.zeros_like(rows[:, :128])
        for x in range(8):
            source = rows[:, 128 * (x // 2) : 128 * (x // 2) + 128]
            moved = shift(source, stride * x + first - (64 * (x % 2) + 8 * y))
            low = stride * x + first
            total = jnp.where((lane >= low) & (lane < low + 8), moved, total)
        store(y, total)


def remote(src, dst, send, recv, device):
    return pltpu.make_async_remote_copy(
        src_ref=src,
        dst_ref=dst,
        send_sem=send,
        recv_sem=recv,
        device_id=device,
        device_id_type=MESH,
    )


STEPS = [(a, b) for a in (-1, 0, 1) for b in (-1, 0, 1) if (a, b) != (0, 0)]


def halo_kernel(vof_ref, nbr_ref, table_ref, lookup_ref, own, send_sem, recv_sem):
    slab = lax.axis_index("stream")
    cross = lax.axis_index("cross")
    partner = [
        (lax.rem(slab + a + SLABS, SLABS), lax.rem(cross + b + CROSS, CROSS)) for a, b in STEPS
    ]
    barrier = pltpu.get_barrier_semaphore()
    for device in partner:
        pl.semaphore_signal(barrier, inc=1, device_id=device, device_id_type=MESH)

    def keep(y, tile):
        own[pl.ds(y, HOME, stride=8), :] = tile

    spread(vof_ref[...].astype(F32), keep, 12, 2)
    table_ref[4] = own[...].astype(BF16)

    pl.semaphore_wait(barrier, len(STEPS))
    copies = []
    for k, (a, b) in enumerate(STEPS):
        copy = remote(
            table_ref.at[4],
            table_ref.at[(1 - a) * 3 + 1 - b],
            send_sem.at[k],
            recv_sem.at[len(STEPS) - 1 - k],
            partner[k],
        )
        copy.start()
        copies.append(copy)

    nbr = nbr_ref[...]
    device = (nbr * 43691) >> 19
    slot = nbr - 12 * device
    place = (((device >> 5) - slab + 1) * 3 + ((device & 31) - cross + 1)) * HOME + slot
    lookup_ref[...] = jnp.where(nbr < 0, 9 * HOME, place)

    for copy in copies:
        copy.wait_send()
    for k, (a, b) in enumerate(STEPS):
        remote(
            table_ref.at[4],
            table_ref.at[(1 + a) * 3 + 1 + b],
            send_sem.at[k],
            recv_sem.at[k],
            partner[k],
        ).wait_recv()


def dot_t(a, b):
    return lax.dot_general(a, b, (((0,), (0,)), ((), ())), preferred_element_type=F32)


def dot_n(a, b):
    return lax.dot_general(a, b, (((1,), (1,)), ((), ())), preferred_element_type=F32)


def dot(a, b):
    return jnp.dot(a, b, preferred_element_type=F32)


def build_first(w1_ref, w1p, t):
    w1p[...] = jnp.zeros_like(w1p)
    w1p[0:125, :] = w1_ref[...].astype(F32)
    w1 = w1p[...].astype(BF16)
    k = lax.broadcasted_iota(jnp.int32, (WIN, 128), 0)
    f = lanes((WIN, 128))
    m = k & 63
    ax = (m * 43) >> 9
    zp = m - 12 * ax
    ay = k >> 6
    code = jnp.where((m < 60) & (ay < 5), 25 * ax + 5 * ay + zp, -1000)
    for z in range(8):
        hit = (f == code - z) & (zp >= z) & (zp < z + 5)
        select = jnp.where(hit, 1.0, 0.0).astype(BF16)
        t[:, 128 * z : 128 * z + 128] = dot(select, w1).astype(BF16)


def build_window(b, lookup_ref, tab, pad, xs):
    lane = lanes((8, 128))
    zp = lane - 12 * ((lane * 43) >> 9)
    for dy in range(3):
        row = []
        for dx in range(3):
            got = []
            for dz in range(3):
                k = 9 * dx + 3 * dy + dz
                if k == 13:
                    at = 4 * HOME + b
                else:
                    at = lookup_ref[b, k if k < 13 else k - 1]
                got.append(tab[pl.ds(pl.multiple_of(at * 8, 8), 8), :])
            row.append(
                jnp.where(zp < 2, shift(got[0], -8), jnp.where(zp < 10, got[1], shift(got[2], 8)))
            )
        low = jnp.where(lane < 24, shift(row[0], -72), shift(row[1], 24))
        high = jnp.where(lane < 72, shift(row[1], -24), shift(row[2], 72))
        pad[0, 8 * dy : 8 * dy + 8, :] = low
        pad[1, 8 * dy : 8 * dy + 8, :] = high
    for half in range(2):
        a = [pad[half, 6 + ay : 14 + ay, :] for ay in range(5)]
        odd = [shift(a[1], 64), shift(a[3], 64)]
        made = []
        for x in range(4):
            inside = (lane >= 12 * x) & (lane < 12 * x + 64)
            made.append(
                [
                    shift(jnp.where(inside, a[0], odd[0]), -12 * x),
                    shift(jnp.where(inside, a[2], odd[1]), -12 * x),
                    shift(a[4], -12 * x),
                ]
            )
        for pair in range(2):
            for g in range(3):
                both = jnp.concatenate([made[2 * pair][g], made[2 * pair + 1][g]], axis=0)
                base = pl.multiple_of(64 * b, 64) + 32 * half + 16 * pair
                xs[pl.ds(pl.multiple_of(base, 16), 16), 128 * g : 128 * g + 128] = both.astype(BF16)


CHUNK = 256


def local_kernel(
    lookup_ref,
    live_ref,
    table_ref,
    target_ref,
    w1_ref,
    wmid_ref,
    wlast_ref,
    grad_ref,
    extra_ref,
    home_ref,
    tab,
    tt,
    pad,
    xs,
    w1p,
    t,
    bd2,
    bd3,
    wle,
    h1,
    h2,
    h3,
    d1,
    d2,
    d3,
    r2,
    pt,
    flat,
    sums,
):
    for i in range(9):
        tab[96 * i : 96 * i + 96, :] = table_ref[i].astype(F32)
    tab[864:872, :] = jnp.zeros((8, 128), F32)

    def keep(y, tile):
        tt[pl.ds(y, HOME, stride=8), :] = tile

    spread(target_ref[...].astype(F32), keep, 8, 0)
    build_first(w1_ref, w1p, t)
    for ref, i in ((bd2, 0), (bd3, 1)):
        ref[...] = jnp.zeros_like(ref)
        ref[0:128, 0:128] = wmid_ref[i]
        ref[128:256, 128:256] = wmid_ref[i]
    wl = wlast_ref[...].astype(F32)
    sub = lax.broadcasted_iota(jnp.int32, (128, 128), 0)
    for z in range(8):
        wle[:, 128 * z : 128 * z + 128] = jnp.where((sub & 7) == z, wl, 0.0).astype(BF16)

    @pl.loop(0, HOME)
    def _(b):
        build_window(b, lookup_ref, tab, pad, xs)

    live = live_ref[0]
    lane = lanes((8, 128))

    @pl.loop(0, ROWS // CHUNK)
    def _(c):
        at = pl.ds(pl.multiple_of(c * CHUNK, CHUNK), CHUNK)
        x = xs[at, :]
        predicted = jnp.zeros((CHUNK, 128), F32)
        for j in range(4):
            col = slice(256 * j, 256 * j + 256)
            a = jnp.tanh(dot(x, t[:, col])).astype(BF16)
            h1[at, col] = a
            a = jnp.tanh(dot(a, bd2[...])).astype(BF16)
            h2[at, col] = a
            a = jnp.tanh(dot(a, bd3[...])).astype(BF16)
            h3[at, col] = a
            predicted += dot_n(a, wle[:, col])
        for i in range(CHUNK // 64):
            b = c * (CHUNK // 64) + i
            tile = jnp.zeros((8, 128), F32)
            for k in range(8):
                part = predicted[64 * i + 8 * k : 64 * i + 8 * k + 8]
                tile = jnp.where(((lane >> 3) & 7) == k, part, tile)
            rows = pl.ds(pl.multiple_of(b * 8, 8), 8)
            mask = jnp.where(b < live, 1.0, 0.0).astype(F32)
            pt[rows, :] = tile
            res = ((tile * mask - tt[rows, :]) * mask / SCALE).astype(BF16).astype(F32)
            for k in range(4):
                both = jnp.concatenate(
                    [
                        jnp.where((lane >> 3) == 2 * k, res, 0.0),
                        jnp.where((lane >> 3) == 2 * k + 1, res, 0.0),
                    ],
                    axis=0,
                )
                r2[pl.ds(pl.multiple_of(b * 64 + 16 * k, 16), 16), :] = both.astype(BF16)
        rr = r2[at, :]
        for j in range(4):
            col = slice(256 * j, 256 * j + 256)
            h = h3[at, col].astype(F32)
            d = (dot(rr, wle[:, col]) * (1.0 - h * h)).astype(BF16)
            d3[at, col] = d
            h = h2[at, col].astype(F32)
            d = (dot_n(d, bd3[...]) * (1.0 - h * h)).astype(BF16)
            d2[at, col] = d
            h = h1[at, col].astype(F32)
            d = (dot_n(d, bd2[...]) * (1.0 - h * h)).astype(BF16)
            d1[at, col] = d

    for b in range(KEEP):
        mask = jnp.where(b < live, 1.0, 0.0).astype(F32)
        home_ref[8 * b : 8 * b + 8, :] = pt[8 * b : 8 * b + 8, :] * mask
    for i in range(3):
        at = 8 * (KEEP + 2 * i)
        extra_ref[i] = jnp.where(lane < 64, pt[at : at + 8, :], pt[at + 8 : at + 16, :])

    second = jnp.zeros((128, 128), F32)
    third = jnp.zeros((128, 128), F32)
    for z in range(8):
        col = slice(128 * z, 128 * z + 128)
        second += dot_t(h1[:, col], d2[:, col])
        third += dot_t(h2[:, col], d3[:, col])
    flat[0:128, :] = second
    flat[128:256, :] = third
    total = jnp.zeros((WIN, 128), F32)
    xv = xs[...]
    for j in range(4):
        g = dot_t(xv, d1[:, 256 * j : 256 * j + 256])
        for i in range(2):
            z = 2 * j + i
            part = g[:, 128 * i : 128 * i + 128]
            total += part if z == 0 else pltpu.roll(part, WIN - z, 0)
    sums[...] = total
    for ax in range(5):
        for ay in range(5):
            at = 64 * ay + 12 * ax
            to = 256 + 25 * ax + 5 * ay
            flat[to : to + 5, :] = sums[at : at + 5, :]
    last = jnp.zeros((1, 128), F32)
    for j in range(4):
        g = dot_t(r2[...], h3[:, 256 * j : 256 * j + 256])
        for i in range(2):
            z = 2 * j + i
            part = jnp.where((sub & 7) == z, g[:, 128 * i : 128 * i + 128], 0.0)
            last += jnp.sum(part, axis=0, keepdims=True)
    flat[381:382, :] = last
    flat[382:384, :] = jnp.zeros((2, 128), F32)
    for i in range(PLANE):
        grad_ref[i] = flat[PIECE * i : PIECE * i + PIECE, :]


def sum_kernel(
    pick_ref,
    grad_ref,
    extra_ref,
    home_ref,
    pred_ref,
    gfirst_ref,
    gmid_ref,
    glast_ref,
    rs,
    lo,
    hi,
    ag,
    eb,
    pk,
    ob,
    rb,
    pt,
    flat,
    rs_s,
    rs_r,
    ag_s,
    ag_r,
    lo_s,
    lo_r,
    hi_s,
    hi_r,
    eb_s,
    eb_r,
    pk_s,
    pk_r,
    ob_s,
    ob_r,
):
    slab = lax.axis_index("stream")
    cross = lax.axis_index("cross")
    zlo, y = slab // 4, lax.rem(slab, 4)
    zhi, xc = cross // 8, lax.rem(cross, 8)
    me = y * 8 + xc

    def of_plane(p):
        return (zlo * 4 + p // 8, zhi * 8 + lax.rem(p, 8))

    def of_lo(q):
        return (q * 4 + y, cross)

    def of_hi(q):
        return (slab, q * 8 + xc)

    def of_row(q):
        return (slab, zhi * 8 + q)

    def others(number, mine, body):
        def step(k, carry):
            body(k, lax.rem(mine + k, number))
            return carry

        lax.fori_loop(1, number, step, 0)

    barrier = pltpu.get_barrier_semaphore()

    def greet(place):
        def body(k, q):
            pl.semaphore_signal(barrier, inc=1, device_id=place(q), device_id_type=MESH)

        return body

    others(PLANE, me, greet(of_plane))
    others(4, zlo, greet(of_lo))
    others(4, zhi, greet(of_hi))

    lane = lanes((8, 128))
    pk[zhi] = jnp.where(lane < 64, pick_ref[0, 0], pick_ref[0, 1])
    rs[me] = grad_ref[me]
    eb[xc] = extra_ref[...]

    pl.semaphore_wait(barrier, PLANE - 1 + 3 + 3)

    def plane_copy(k, q, slot):
        return remote(grad_ref.at[q], rs.at[slot], rs_s.at[k], rs_r.at[slot], of_plane(q))

    def row_copy(k, q, slot):
        return remote(extra_ref, eb.at[slot], eb_s.at[k], eb_r.at[slot], of_row(q))

    def pick_copy(k, q, slot):
        return remote(pk.at[zhi], pk.at[slot], pk_s.at[k], pk_r.at[slot], of_hi(q))

    def lo_copy(k, q, slot):
        return remote(lo.at[zlo], lo.at[slot], lo_s.at[k], lo_r.at[slot], of_lo(q))

    def hi_copy(k, q, slot):
        return remote(hi.at[zhi], hi.at[slot], hi_s.at[k], hi_r.at[slot], of_hi(q))

    def out_copy(k, q, slot):
        return remote(ob.at[q], rb.at[slot], ob_s.at[k], ob_r.at[slot], of_hi(q))

    def all_copy(k, q, slot):
        return remote(ag.at[me], ag.at[slot], ag_s.at[k], ag_r.at[slot], of_plane(q))

    def start(number, mine, copy):
        others(number, mine, lambda k, q: copy(k, q, mine).start())

    def arrive(number, mine, copy):
        others(number, mine, lambda k, q: copy(k, q, q).wait_recv())

    def sent(number, mine, copy):
        others(number, mine, lambda k, q: copy(k, q, mine).wait_send())

    start(PLANE, me, plane_copy)
    start(4, zhi, pick_copy)
    start(8, xc, row_copy)

    arrive(PLANE, me, plane_copy)
    total = rs[0]
    for i in range(1, PLANE):
        total += rs[i]
    lo[zlo] = total
    start(4, zlo, lo_copy)

    arrive(4, zhi, pick_copy)
    arrive(8, xc, row_copy)
    outs = [jnp.zeros((8, 128), F32) for _ in range(4)]
    wants = [pk[q] for q in range(4)]
    for d in range(8):
        for i in range(3):
            tile = eb[d, i]
            swapped = shift(tile, 64)
            name = (zhi * 8 + d) * KEEP + 2 * i
            first = jnp.where(lane < 64, tile, swapped)
            other = jnp.where(lane < 64, swapped, tile)
            for q in range(4):
                outs[q] = jnp.where(wants[q] == name, first, outs[q])
                outs[q] = jnp.where(wants[q] == name + 1, other, outs[q])
    for q in range(4):
        ob[q] = outs[q]
    start(4, zhi, out_copy)
    rb[zhi] = ob[zhi]

    arrive(4, zlo, lo_copy)
    hi[zhi] = (lo[0] + lo[1]) + (lo[2] + lo[3])
    start(4, zhi, hi_copy)

    arrive(4, zhi, out_copy)
    tile = (rb[0] + rb[1]) + (rb[2] + rb[3])
    pt[0:48, :] = home_ref[...]
    pt[48:56, :] = tile
    pt[56:64, :] = shift(tile, 64)
    parts = [jnp.zeros((8, 128), F32) for _ in range(4)]
    for yy in range(8):
        v = pt[pl.ds(yy, 8, stride=8), :]
        for x in range(8):
            low = 64 * (x % 2) + 8 * yy
            inside = (lane >= low) & (lane < low + 8)
            parts[x // 2] = jnp.where(inside, shift(v, low - 8 * x), parts[x // 2])
    for i in range(4):
        pred_ref[:, 128 * i : 128 * i + 128] = parts[i]

    arrive(4, zhi, hi_copy)
    ag[me] = (hi[0] + hi[1]) + (hi[2] + hi[3])
    start(PLANE, me, all_copy)
    sent(PLANE, me, plane_copy)
    sent(8, xc, row_copy)
    sent(4, zhi, pick_copy)
    sent(4, zlo, lo_copy)
    sent(4, zhi, out_copy)
    sent(4, zhi, hi_copy)
    arrive(PLANE, me, all_copy)
    for i in range(PLANE):
        flat[PIECE * i : PIECE * i + PIECE, :] = ag[i]
    gmid_ref[0] = flat[0:128, :]
    gmid_ref[1] = flat[128:256, :]
    gfirst_ref[...] = flat[256:381, :]
    glast_ref[...] = flat[381:382, :]
    sent(PLANE, me, all_copy)


def dma(n):
    return pltpu.SemaphoreType.DMA((n,))


def halo(vof, neighbours):
    return pl.pallas_call(
        halo_kernel,
        out_shape=(
            jax.ShapeDtypeStruct((9, 96, 128), BF16),
            jax.ShapeDtypeStruct((HOME, 26), jnp.int32),
        ),
        in_specs=[VMEM, VMEM],
        out_specs=(VMEM, VMEM),
        scratch_shapes=[pltpu.VMEM((96, 128), F32), dma(8), dma(8)],
        compiler_params=pltpu.CompilerParams(
            collective_id=0, has_side_effects=True, vmem_limit_bytes=16 << 20
        ),
        name="halo",
    )(vof, neighbours)


def local_terms(lookup, live_blocks, table, target, w_first, w_mid, w_last):
    big = pltpu.VMEM((ROWS, 1024), BF16)
    return pl.pallas_call(
        local_kernel,
        out_shape=(
            jax.ShapeDtypeStruct((PLANE, PIECE, 128), F32),
            jax.ShapeDtypeStruct((3, 8, 128), F32),
            jax.ShapeDtypeStruct((48, 128), F32),
        ),
        in_specs=[SMEM, SMEM, VMEM, VMEM, VMEM, VMEM, VMEM],
        out_specs=(VMEM, VMEM, VMEM),
        scratch_shapes=[
            pltpu.VMEM((872, 128), F32),
            pltpu.VMEM((96, 128), F32),
            pltpu.VMEM((2, 24, 128), F32),
            pltpu.VMEM((ROWS, WIN), BF16),
            pltpu.VMEM((128, 128), F32),
            pltpu.VMEM((WIN, 1024), BF16),
            pltpu.VMEM((256, 256), BF16),
            pltpu.VMEM((256, 256), BF16),
            pltpu.VMEM((128, 1024), BF16),
            big,
            big,
            big,
            big,
            big,
            big,
            pltpu.VMEM((ROWS, 128), BF16),
            pltpu.VMEM((96, 128), F32),
            pltpu.VMEM((384, 128), F32),
            pltpu.VMEM((384, 128), F32),
        ],
        compiler_params=pltpu.CompilerParams(vmem_limit_bytes=40 << 20),
        name="local_terms",
    )(lookup, live_blocks, table, target, w_first, w_mid, w_last)


def sum_all(pick, grads, extra, home):
    piece = pltpu.VMEM((PLANE, PIECE, 128), F32)
    small = pltpu.VMEM((4, PIECE, 128), F32)
    return pl.pallas_call(
        sum_kernel,
        out_shape=(
            jax.ShapeDtypeStruct((8, 512), F32),
            jax.ShapeDtypeStruct((125, 128), F32),
            jax.ShapeDtypeStruct((2, 128, 128), F32),
            jax.ShapeDtypeStruct((1, 128), F32),
        ),
        in_specs=[SMEM, VMEM, VMEM, VMEM],
        out_specs=(VMEM, VMEM, VMEM, VMEM),
        scratch_shapes=[
            piece,
            small,
            small,
            piece,
            pltpu.VMEM((8, 3, 8, 128), F32),
            pltpu.VMEM((4, 8, 128), jnp.int32),
            pltpu.VMEM((4, 8, 128), F32),
            pltpu.VMEM((4, 8, 128), F32),
            pltpu.VMEM((64, 128), F32),
            pltpu.VMEM((384, 128), F32),
            dma(PLANE),
            dma(PLANE),
            dma(PLANE),
            dma(PLANE),
            dma(4),
            dma(4),
            dma(4),
            dma(4),
            dma(8),
            dma(8),
            dma(4),
            dma(4),
            dma(4),
            dma(4),
        ],
        compiler_params=pltpu.CompilerParams(
            collective_id=1, has_side_effects=True, vmem_limit_bytes=16 << 20
        ),
        name="sum_all",
    )(pick, grads, extra, home)


def shards(vof, target, neighbours, live_blocks, pick, w_first, w_mid, w_last):
    table, lookup = halo(vof, neighbours)
    grads, extra, home = local_terms(
        lookup, live_blocks, table, target, w_first, w_mid, w_last.reshape(1, 128)
    )
    pred, gfirst, gmid, glast = sum_all(pick, grads, extra, home)
    return pred, gfirst, gmid, glast.reshape(128)


def solution(mesh):
    both = ("stream", "cross")
    return jax.shard_map(
        shards,
        mesh=mesh,
        in_specs=(
            P(both, None),
            P(both, None),
            P(both, None),
            P(both),
            P(both, None),
            P(),
            P(),
            P(),
        ),
        out_specs=(P(both, None), P(), P(), P()),
        check_vma=False,
    )
```

time: 803 us -> 78.8 us (0.10)
  waiting for transfers between devices: 455 us -> 0 us
  local copies, waits for them, and re-layouts: 152 us -> 6.7 us
  blocking collectives: 114 us -> 0 us
  Pallas kernels: 0 us -> 70.3 us
  other arithmetic: 39.4 us -> 0 us
  between operations: 17.8 us -> 1.33 us
  matrix products: 9.76 us -> 0 us
  starting transfers between devices: 9.69 us -> 0 us
    psum x1 -> x0, waiting for transfers between devices: 455 us -> none  [shards(): summed = lax.psum(packed, ('stream', 'cross'))]
    all_gather x2 -> x0, blocking collectives: 114 us -> none  [the longest x1 60.5 us: shards(): lax.all_gather(target[KEEP:], 'cross', axis=0, tiled=True)]
    another operation x127 -> x0, local copies, waits for them, and re-layouts: 77.5 us -> none  [the longest x126 77.5 us: stencil(): return jnp.stack(columns)]
    pallas_call x0 -> x3, Pallas kernels: none -> 70.3 us  [the longest x1 32.3 us: sum_all(): pl.pallas_call(sum_kernel, out_shape=(jax.ShapeDtypeStruct((8, 512), F32)...]
    slice x131 -> x0, local copies, waits for them, and re-layouts: 44.8 us -> none  [the longest x125 38.1 us: stencil(): padded[:, along_x:along_x + block_edge, along_y:along_y + block_edge, alo...]
    concatenate x34 -> x0, other arithmetic: 35.9 us -> none  [the longest x31 34.8 us: shards(): work_padded = jnp.concatenate([padded[:KEEP], got_blocks], axis=0)]
    transpose x1 -> x0, local copies, waits for them, and re-layouts: 12.7 us -> none  [assemble(): shaped.transpose(0, 1, 4, 2, 5, 3, 6)]
    dot_general x11 -> x0, matrix products: 9.76 us -> none  [the longest x3 4.92 us: contract_cols(): lax.dot_general(former, latter, (((1,), (1,)), ((), ())), preferred_eleme...]
  transfers between devices with their start and end apart: 5 -> 0, of which waited for: 1 -> 0; matrix products, arithmetic and copies ran while one was open for 1% -> 0% of each run, Pallas kernels for 0% -> 0%
where the time goes in v1:
time: 78.8 us; the launch traced here: 78.4 us
  Pallas kernels  70.3 us (89%)
  local copies, waits for them, and re-layouts  6.7 us (9%)
  between operations  1.33 us (2%)
    pallas_call x1, Pallas kernels, sum_all(): pl.pallas_call(sum_kernel, out_shape=(jax.ShapeDtypeStruct((8, 512), F32)...  32.3 us
    pallas_call x1, Pallas kernels, halo(): pl.pallas_call(halo_kernel, out_shape=(jax.ShapeDtypeStruct((9, 96, 128),...  22.5 us
    pallas_call x1, Pallas kernels, local_terms(): pl.pallas_call(local_kernel, out_shape=(jax.ShapeDtypeStruct((PLANE, PIEC...  15.4 us
    unnamed x18, local copies, waits for them, and re-layouts  6.7 us

profile of v1, /device:TPU:1, one launch (start us, length us, event | category | flops | bytes accessed | tf_op | source)
XLA Modules:
  0.0 78.4 jit_solution(18401429913194680478)
XLA Ops:
  1.3 0.0 copy-start.2
  1.3 0.7 copy-done.2
  2.0 0.0 copy-start.4
  2.0 0.7 copy-done.4
  2.7 0.0 copy-start.3
  2.7 22.5 %halo.1 = (bf16[9,96,128]{2,1,0:T(8,128)(2,1)S(1)}, s32[12,26]{1,0:T(8,128)S(1)}) custom-call(bf16[12,512]{1,0:T(8,128)(2,1)S(1)} %copy-done.2, s32[12,26]{1,0:T(8,128)S(1)} %copy-done.4), custom_call_target="tpu_custom_call" | custom-call | tf_op jit(solution)/shard_map/halo/pallas_call | solution.py:505
  25.2 0.0 copy-start.5
  25.3 0.0 copy-done.3
  25.3 0.6 copy-done.5
  25.9 0.0 copy-start
  25.9 0.8 %copy-done = bf16[2,128,128]{2,1,0:T(8,128)(2,1)S(1)} copy-done((bf16[2,128,128]{2,1,0:T(8,128)(2,1)S(1)}, bf16[2,128,128]{2,1,0:T(8,128)(2,1)}, u32[]{:S(2)}) %copy-start) | copy-done | bytes 65560
  26.7 0.0 copy-start.1
  26.7 0.8 copy-done.1
  27.5 15.4 %local_terms.1 = (f32[32,12,128]{2,1,0:T(8,128)S(1)}, f32[3,8,128]{2,1,0:T(8,128)S(1)}, f32[48,128]{1,0:T(8,128)S(1)}) custom-call(s32[12,26]{1,0:T(8,128)S(1)} %get-tuple-element.13.lookup_ref, s32[1]{0:T(128)S(6)} %copy.16.live_ref, bf16[9,96,128]{2,1,0:T(8,128)(2,1)S(1)} %get-tuple-element.14.table_ref, bf16[12,512]{1,0:T(8,128)(2,1)S(1)} %copy-done.3, ...), custom_call_target="tpu_custom_call" | custom-call | tf_op jit(solution)/shard_map/local_terms/pallas_call | solution.py:523
  42.9 0.0 copy-start.6
  43.0 0.6 copy-done.6
  43.6 32.3 %sum_all.1 = (f32[8,512]{1,0:T(8,128)S(1)}, f32[125,128]{1,0:T(8,128)S(1)}, f32[2,128,128]{2,1,0:T(8,128)S(1)}, f32[1,128]{1,0:T(1,128)S(1)}) custom-call(s32[1,2]{1,0:T(1,128)S(1)} %copy-done.6, f32[32,12,128]{2,1,0:T(8,128)S(1)} %get-tuple-element.15.grad_ref, f32[3,8,128]{2,1,0:T(8,128)S(1)} %get-tuple-element.16.extra_ref, ...), custom_call_target="tpu_custom_call" | custom-call | tf_op jit(solution)/shard_map/sum_all/pallas_call | solution.py:561
  76.0 0.6 copy.17
  76.6 0.6 copy.18
  77.2 0.7 copy.19
  77.9 0.5 copy.20
Async XLA Ops:
  1.3 0.7 copy-start.2
  2.0 0.7 copy-start.4
  2.7 22.6 %copy-start.3 = (bf16[12,512]{1,0:T(8,128)(2,1)S(1)}, bf16[12,512]{1,0:T(8,128)(2,1)}, u32[]{:S(2)}) copy-start(bf16[12,512]{1,0:T(8,128)(2,1)} %target_ref.1) | copy-start | bytes 36868
  25.2 0.7 copy-start.5
  25.9 0.8 %copy-start = (bf16[2,128,128]{2,1,0:T(8,128)(2,1)S(1)}, bf16[2,128,128]{2,1,0:T(8,128)(2,1)}, u32[]{:S(2)}) copy-start(bf16[2,128,128]{2,1,0:T(8,128)(2,1)} %wmid_ref.1) | copy-start | bytes 196612
  26.7 0.8 copy-start.1
  42.9 0.7 copy-start.6

commit v2 on v1

v2 whole, which is shorter than its diff:
```python
import jax
import jax.numpy as jnp
from jax import lax
from jax.experimental import pallas as pl
from jax.experimental.pallas import tpu as pltpu
from jax.sharding import PartitionSpec as P

MESH = pl.DeviceIdType.MESH
F32 = jnp.float32
BF16 = jnp.bfloat16

KEEP = 6
HOME = 12
ROWS = 768
WIN = 384
SCALE = 1572864.0
SLABS = 16
CROSS = 32
PIECE = 12
VMEM = pl.BlockSpec(memory_space=pltpu.VMEM)


def lanes(shape):
    return lax.broadcasted_iota(jnp.int32, shape, len(shape) - 1)


def shift(x, by):
    by = by % 128
    return x if by == 0 else pltpu.roll(x, by, x.ndim - 1)


def spread(parts, store, stride, first):
    lane = lanes(parts[0].shape)
    for y in range(8):
        total = jnp.zeros_like(parts[0])
        for x in range(8):
            moved = shift(parts[x // 2], stride * x + first - (64 * (x % 2) + 8 * y))
            low = stride * x + first
            total = jnp.where((lane >= low) & (lane < low + 8), moved, total)
        store(y, total)


def keep_in(ref):
    def store(y, tile):
        ref[pl.ds(y, HOME, stride=8), :] = tile

    return store


def remote(src, dst, send, recv, device):
    return pltpu.make_async_remote_copy(
        src_ref=src,
        dst_ref=dst,
        send_sem=send,
        recv_sem=recv,
        device_id=device,
        device_id_type=MESH,
    )


def dot_t(a, b):
    return lax.dot_general(a, b, (((0,), (0,)), ((), ())), preferred_element_type=F32)


def dot_n(a, b):
    return lax.dot_general(a, b, (((1,), (1,)), ((), ())), preferred_element_type=F32)


def dot(a, b):
    return jnp.dot(a, b, preferred_element_type=F32)


def build_first(w1_ref, w1p, t):
    w1p[...] = jnp.zeros_like(w1p)
    w1p[0:125, :] = w1_ref[...].astype(F32)
    w1 = w1p[...].astype(BF16)
    k = lax.broadcasted_iota(jnp.int32, (WIN, 128), 0)
    f = lanes((WIN, 128))
    m = k & 63
    ax = (m * 43) >> 9
    zp = m - 12 * ax
    ay = k >> 6
    code = jnp.where((m < 60) & (ay < 5), 25 * ax + 5 * ay + zp, -1000)
    for z in range(8):
        hit = (f == code - z) & (zp >= z) & (zp < z + 5)
        select = jnp.where(hit, 1.0, 0.0).astype(BF16)
        t[:, 128 * z : 128 * z + 128] = dot(select, w1).astype(BF16)


def build_window(b, lookup_ref, tab, pad, xs):
    lane = lanes((8, 128))
    zp = lane - 12 * ((lane * 43) >> 9)
    for dy in range(3):
        row = []
        for dx in range(3):
            got = []
            for dz in range(3):
                k = 9 * dx + 3 * dy + dz
                if k == 13:
                    at = 4 * HOME + b
                else:
                    at = lookup_ref[b, k if k < 13 else k - 1]
                got.append(tab[at])
            row.append(
                jnp.where(zp < 2, shift(got[0], -8), jnp.where(zp < 10, got[1], shift(got[2], 8)))
            )
        low = jnp.where(lane < 24, shift(row[0], -72), shift(row[1], 24))
        high = jnp.where(lane < 72, shift(row[1], -24), shift(row[2], 72))
        pad[0, 8 * dy : 8 * dy + 8, :] = low
        pad[1, 8 * dy : 8 * dy + 8, :] = high
    for half in range(2):
        a = [pad[half, 6 + ay : 14 + ay, :] for ay in range(5)]
        odd = [shift(a[1], 64), shift(a[3], 64)]
        made = []
        for x in range(4):
            inside = (lane >= 12 * x) & (lane < 12 * x + 64)
            made.append(
                [
                    shift(jnp.where(inside, a[0], odd[0]), -12 * x),
                    shift(jnp.where(inside, a[2], odd[1]), -12 * x),
                    shift(a[4], -12 * x),
                ]
            )
        for pair in range(2):
            for g in range(3):
                both = jnp.concatenate([made[2 * pair][g], made[2 * pair + 1][g]], axis=0)
                base = pl.multiple_of(64 * b, 64) + 32 * half + 16 * pair
                xs[pl.ds(pl.multiple_of(base, 16), 16), 128 * g : 128 * g + 128] = both.astype(BF16)


STEPS = [(a, b) for a in (-1, 0, 1) for b in (-1, 0, 1) if (a, b) != (0, 0)]
STEPS.sort(key=lambda step: (step[1] == 0, step[0] == 0))
CHUNK = 256


def train_kernel(
    vof_hbm,
    target_hbm,
    nbr_hbm,
    live_hbm,
    pick_hbm,
    w1_hbm,
    wmid_hbm,
    wlast_hbm,
    sum_ref,
    pred_ref,
    vof_ref,
    target_ref,
    nbr_ref,
    live_ref,
    pick_ref,
    w1_ref,
    wmid_ref,
    wlast_ref,
    lookup_vec,
    lookup_ref,
    packed,
    table,
    tall,
    tab,
    tt,
    pad,
    xs,
    w1p,
    t,
    bd2,
    bd3,
    wle,
    h1,
    h2,
    h3,
    d1,
    d2,
    d3,
    r2,
    pt,
    flat,
    sums,
    extra,
    eb,
    pk,
    ob,
    rb,
    cs,
    half,
    hs,
    rs,
    zb,
    in_s,
    halo_s,
    halo_r,
    eb_s,
    eb_r,
    pk_s,
    pk_r,
    ob_s,
    ob_r,
    cs_s,
    cs_r,
    rs_s,
    rs_r,
    zb_s,
    zb_r,
    ag_s,
    ag_r,
):
    fetches = [
        pltpu.make_async_copy(src, dst, in_s.at[i])
        for i, (src, dst) in enumerate(
            (
                (vof_hbm, vof_ref),
                (nbr_hbm, nbr_ref),
                (w1_hbm, w1_ref),
                (wmid_hbm, wmid_ref),
                (wlast_hbm, wlast_ref),
                (target_hbm, target_ref),
                (live_hbm, live_ref),
                (pick_hbm, pick_ref),
            )
        )
    ]
    for fetch in fetches:
        fetch.start()

    slab = lax.axis_index("stream")
    cross = lax.axis_index("cross")
    zlo, y = slab // 4, lax.rem(slab, 4)
    zhi, xc = cross // 8, lax.rem(cross, 8)
    x, core = xc // 2, lax.rem(xc, 2)
    zz = zhi * 4 + zlo
    xy = y * 4 + x
    pair = (slab, cross + 1 - 2 * core)

    def of_xy(q):
        return (zlo * 4 + q // 4, zhi * 8 + 2 * lax.rem(q, 4) + core)

    def of_z(q):
        return (lax.rem(q, 4) * 4 + y, (q // 4) * 8 + xc)

    def of_hi(q):
        return (slab, q * 8 + xc)

    def of_row(q):
        return (slab, zhi * 8 + q)

    def others(number, mine, body):
        def step(k, carry):
            body(k, lax.rem(mine + k, number))
            return carry

        lax.fori_loop(1, number, step, 0)

    table[...] = jnp.zeros_like(table)

    barrier = pltpu.get_barrier_semaphore()

    def greet(device):
        pl.semaphore_signal(barrier, inc=1, device_id=device, device_id_type=MESH)

    others(16, zz, lambda k, q: greet(of_z(q)))
    near = []
    count = jnp.int32(15 + 15 + 7 + 1)
    for a, b in STEPS:
        valid = (slab + a >= 0) & (slab + a < SLABS) & (cross + b >= 0) & (cross + b < CROSS)
        device = (lax.rem(slab + a + SLABS, SLABS), lax.rem(cross + b + CROSS, CROSS))
        near.append((valid, device))
        count += jnp.where(valid, 1, 0)

        @pl.when(valid)
        def _():
            greet(device)

    others(16, xy, lambda k, q: greet(of_xy(q)))
    others(8, xc, lambda k, q: greet(of_row(q)))
    greet(pair)

    fetches[0].wait()
    rows = vof_ref[...].astype(F32)
    for i in range(4):
        packed[HOME * i : HOME * i + HOME, :] = rows[:, 128 * i : 128 * i + 128]
    table[4] = packed[...].astype(BF16)

    pl.semaphore_wait(barrier, count)

    def halo_copy(k, slot, sem):
        return remote(table.at[4], table.at[slot], halo_s.at[k], halo_r.at[sem], near[k][1])

    def slot_of(a, b):
        return (1 + a) * 3 + 1 + b

    for k, (a, b) in enumerate(STEPS):

        @pl.when(near[k][0])
        def _():
            halo_copy(k, slot_of(-a, -b), STEPS.index((-a, -b))).start()

    fetches[7].wait()
    lane = lanes((8, 128))
    pick = pick_ref[...]
    pk[zhi] = jnp.where(
        lane < 64,
        jnp.broadcast_to(pick[:, 0:1], (8, 128)),
        jnp.broadcast_to(pick[:, 1:2], (8, 128)),
    )

    def row_copy(k, q, slot):
        return remote(extra, eb.at[slot], eb_s.at[k], eb_r.at[slot], of_row(q))

    def pick_copy(k, q, slot):
        return remote(pk.at[zhi], pk.at[slot], pk_s.at[k], pk_r.at[slot], of_hi(q))

    def out_copy(k, q, slot):
        return remote(ob.at[q], rb.at[slot], ob_s.at[k], ob_r.at[slot], of_hi(q))

    def xy_copy(k, q, slot):
        return remote(hs.at[q], rs.at[slot], rs_s.at[k], rs_r.at[slot], of_xy(q))

    def z_copy(k, q, slot):
        return remote(zb.at[zz], zb.at[slot], zb_s.at[k], zb_r.at[slot], of_z(q))

    def all_copy(k, q, slot):
        return remote(
            sum_ref.at[core, xy], sum_ref.at[core, slot], ag_s.at[k], ag_r.at[slot], of_xy(q)
        )

    def start(number, mine, copy):
        others(number, mine, lambda k, q: copy(k, q, mine).start())

    def arrive(number, mine, copy):
        others(number, mine, lambda k, q: copy(k, q, q).wait_recv())

    def sent(number, mine, copy):
        others(number, mine, lambda k, q: copy(k, q, mine).wait_send())

    start(4, zhi, pick_copy)

    fetches[1].wait()
    nbr = nbr_ref[...]
    device = (nbr * 43691) >> 19
    slot = nbr - 12 * device
    place = (((device >> 5) - slab + 1) * 3 + ((device & 31) - cross + 1)) * HOME + slot
    place = jnp.clip(place, 0, 9 * HOME - 1)
    lookup_vec[...] = jnp.where(nbr < 0, 9 * HOME, place)
    to_scalar = pltpu.make_async_copy(lookup_vec, lookup_ref, in_s.at[0])
    to_scalar.start()

    fetches[2].wait()
    build_first(w1_ref, w1p, t)
    fetches[3].wait()
    fetches[4].wait()
    for ref, i in ((bd2, 0), (bd3, 1)):
        ref[...] = jnp.zeros_like(ref)
        ref[0:128, 0:128] = wmid_ref[i]
        ref[128:256, 128:256] = wmid_ref[i]
    wl = wlast_ref[...].astype(F32)
    sub = lax.broadcasted_iota(jnp.int32, (128, 128), 0)
    for z in range(8):
        wle[:, 128 * z : 128 * z + 128] = jnp.where((sub & 7) == z, wl, 0.0).astype(BF16)
    fetches[5].wait()
    fetches[6].wait()
    source = target_ref[...].astype(F32)
    spread([source[:, 128 * i : 128 * i + 128] for i in range(4)], keep_in(tt), 8, 0)
    tab[9 * HOME] = jnp.zeros((8, 128), F32)

    def unpack(slot):
        packed[...] = table[slot].astype(F32)
        parts = [packed[HOME * i : HOME * i + HOME, :] for i in range(4)]
        spread(parts, keep_in(tall), 12, 2)
        for i in range(HOME):
            tab[HOME * slot + i] = tall[8 * i : 8 * i + 8, :]

    unpack(4)
    for k in reversed(range(8)):

        @pl.when(near[k][0])
        def _():
            halo_copy(k, slot_of(*STEPS[k]), k).wait_recv()

        unpack(slot_of(*STEPS[k]))

    to_scalar.wait()

    @pl.loop(0, HOME)
    def _(b):
        build_window(b, lookup_ref, tab, pad, xs)

    live = jnp.full((8, 128), live_ref[0], jnp.int32)

    def train(c):
        at = pl.ds(pl.multiple_of(c * CHUNK, CHUNK), CHUNK)
        window = xs[at, :]
        predicted = jnp.zeros((CHUNK, 128), F32)
        for j in range(4):
            col = slice(256 * j, 256 * j + 256)
            a = jnp.tanh(dot(window, t[:, col])).astype(BF16)
            h1[at, col] = a
            a = jnp.tanh(dot(a, bd2[...])).astype(BF16)
            h2[at, col] = a
            a = jnp.tanh(dot(a, bd3[...])).astype(BF16)
            h3[at, col] = a
            predicted += dot_n(a, wle[:, col])
        for i in range(CHUNK // 64):
            b = c * (CHUNK // 64) + i
            tile = jnp.zeros((8, 128), F32)
            for k in range(8):
                part = predicted[64 * i + 8 * k : 64 * i + 8 * k + 8]
                tile = jnp.where(((lane >> 3) & 7) == k, part, tile)
            rows = pl.ds(pl.multiple_of(b * 8, 8), 8)
            mask = jnp.where(b < live, 1.0, 0.0).astype(F32)
            pt[rows, :] = tile
            res = ((tile * mask - tt[rows, :]) * mask / SCALE).astype(BF16).astype(F32)
            for k in range(4):
                both = jnp.concatenate(
                    [
                        jnp.where((lane >> 3) == 2 * k, res, 0.0),
                        jnp.where((lane >> 3) == 2 * k + 1, res, 0.0),
                    ],
                    axis=0,
                )
                r2[pl.ds(pl.multiple_of(b * 64 + 16 * k, 16), 16), :] = both.astype(BF16)
        rr = r2[at, :]
        for j in range(4):
            col = slice(256 * j, 256 * j + 256)
            h = h3[at, col].astype(F32)
            d = (dot(rr, wle[:, col]) * (1.0 - h * h)).astype(BF16)
            d3[at, col] = d
            h = h2[at, col].astype(F32)
            d = (dot_n(d, bd3[...]) * (1.0 - h * h)).astype(BF16)
            d2[at, col] = d
            h = h1[at, col].astype(F32)
            d = (dot_n(d, bd2[...]) * (1.0 - h * h)).astype(BF16)
            d1[at, col] = d

    @pl.loop(0, 3)
    def _(c):
        train(2 - c)

        @pl.when(c == 1)
        def _():
            for i in range(3):
                at = 8 * (KEEP + 2 * i)
                extra[i] = jnp.where(lane < 64, pt[at : at + 8, :], pt[at + 8 : at + 16, :])
            eb[xc] = extra[...]
            start(8, xc, row_copy)

    second = jnp.zeros((128, 128), F32)
    third = jnp.zeros((128, 128), F32)
    for z in range(8):
        col = slice(128 * z, 128 * z + 128)
        second += dot_t(h1[:, col], d2[:, col])
        third += dot_t(h2[:, col], d3[:, col])
    flat[0:128, :] = second
    flat[128:256, :] = third

    arrive(4, zhi, pick_copy)
    arrive(8, xc, row_copy)
    ob[...] = jnp.zeros_like(ob)
    wants = [pk[q] for q in range(4)]

    @pl.loop(0, 8)
    def _(d):
        for i in range(3):
            tile = eb[d, i]
            swapped = shift(tile, 64)
            name = (zhi * 8 + d) * KEEP + 2 * i
            first = jnp.where(lane < 64, tile, swapped)
            other = jnp.where(lane < 64, swapped, tile)
            for q in range(4):
                old = ob[q]
                old = jnp.where(wants[q] == name, first, old)
                ob[q] = jnp.where(wants[q] == name + 1, other, old)

    start(4, zhi, out_copy)
    rb[zhi] = ob[zhi]

    total = jnp.zeros((WIN, 128), F32)
    xv = xs[...]
    for j in range(4):
        g = dot_t(xv, d1[:, 256 * j : 256 * j + 256])
        for i in range(2):
            z = 2 * j + i
            part = g[:, 128 * i : 128 * i + 128]
            total += part if z == 0 else pltpu.roll(part, WIN - z, 0)
    sums[...] = total
    for ax in range(5):
        for ay in range(5):
            at = 64 * ay + 12 * ax
            to = 256 + 25 * ax + 5 * ay
            flat[to : to + 5, :] = sums[at : at + 5, :]
    last = jnp.zeros((1, 128), F32)
    for j in range(4):
        g = dot_t(r2[...], h3[:, 256 * j : 256 * j + 256])
        for i in range(2):
            z = 2 * j + i
            part = jnp.where((sub & 7) == z, g[:, 128 * i : 128 * i + 128], 0.0)
            last += jnp.sum(part, axis=0, keepdims=True)
    flat[381:382, :] = last
    flat[382:384, :] = jnp.zeros((2, 128), F32)

    def half_of(c):
        return flat.at[pl.ds(pl.multiple_of(192 * c, 192), 192)]

    first_pair = remote(half_of(1 - core), cs, cs_s.at[0], cs_r.at[0], pair)
    first_pair.start()
    first_pair.wait_recv()
    half[...] = half_of(core)[...] + cs[...]
    for i in range(16):
        hs[i] = half[PIECE * i : PIECE * i + PIECE, :]
    start(16, xy, xy_copy)
    rs[xy] = hs[xy]
    arrive(16, xy, xy_copy)
    total = rs[0]
    for i in range(1, 16):
        total += rs[i]
    zb[zz] = total
    start(16, zz, z_copy)

    for b in range(KEEP):
        mask = jnp.where(b < live, 1.0, 0.0).astype(F32)
        pred_ref[8 * b : 8 * b + 8, :] = pt[8 * b : 8 * b + 8, :] * mask
    arrive(4, zhi, out_copy)
    tile = (rb[0] + rb[1]) + (rb[2] + rb[3])
    pred_ref[48:56, :] = tile
    pred_ref[56:64, :] = shift(tile, 64)

    for k in range(8):

        @pl.when(near[k][0])
        def _():
            halo_copy(k, 0, k).wait_send()

    sent(4, zhi, pick_copy)
    sent(8, xc, row_copy)
    sent(4, zhi, out_copy)
    first_pair.wait_send()
    sent(16, xy, xy_copy)

    arrive(16, zz, z_copy)
    total = zb[0]
    for i in range(1, 16):
        total += zb[i]
    sum_ref[core, xy] = total
    start(16, xy, all_copy)
    sent(16, zz, z_copy)
    arrive(16, xy, all_copy)
    last_pair = remote(sum_ref.at[core], sum_ref.at[core], cs_s.at[1], cs_r.at[1], pair)
    last_pair.start()
    sent(16, xy, all_copy)
    last_pair.wait_send()
    remote(
        sum_ref.at[1 - core], sum_ref.at[1 - core], cs_s.at[1], cs_r.at[1], pair
    ).wait_recv()


def write_kernel(sum_ref, tile_ref, pred_ref, gfirst_ref, gmid_ref, glast_ref, flat):
    for c in range(2):
        for i in range(16):
            at = 192 * c + PIECE * i
            flat[at : at + PIECE, :] = sum_ref[c, i]
    gmid_ref[0] = flat[0:128, :]
    gmid_ref[1] = flat[128:256, :]
    gfirst_ref[...] = flat[256:381, :]
    glast_ref[...] = flat[381:382, :]
    lane = lanes((8, 128))
    parts = [jnp.zeros((8, 128), F32) for _ in range(4)]
    for y in range(8):
        v = tile_ref[pl.ds(y, 8, stride=8), :]
        for x in range(8):
            low = 64 * (x % 2) + 8 * y
            inside = (lane >= low) & (lane < low + 8)
            parts[x // 2] = jnp.where(inside, shift(v, low - 8 * x), parts[x // 2])
    for i in range(4):
        pred_ref[:, 128 * i : 128 * i + 128] = parts[i]


def dma(n):
    return pltpu.SemaphoreType.DMA((n,))


def train(vof, target, neighbours, live_blocks, pick, w_first, w_mid, w_last):
    big = pltpu.VMEM((ROWS, 1024), BF16)
    piece = pltpu.VMEM((16, PIECE, 128), F32)
    tiles = pltpu.VMEM((4, 8, 128), F32)
    return pl.pallas_call(
        train_kernel,
        out_shape=(
            jax.ShapeDtypeStruct((2, 16, PIECE, 128), F32),
            jax.ShapeDtypeStruct((64, 128), F32),
        ),
        in_specs=[pl.BlockSpec(memory_space=pltpu.HBM)] * 8,
        out_specs=(VMEM, VMEM),
        scratch_shapes=[
            pltpu.VMEM((HOME, 512), BF16),
            pltpu.VMEM((HOME, 512), BF16),
            pltpu.VMEM((HOME, 26), jnp.int32),
            pltpu.SMEM((1,), jnp.int32),
            pltpu.VMEM((1, 2), jnp.int32),
            pltpu.VMEM((125, 128), BF16),
            pltpu.VMEM((2, 128, 128), BF16),
            pltpu.VMEM((1, 128), BF16),
            pltpu.VMEM((HOME, 26), jnp.int32),
            pltpu.SMEM((HOME, 26), jnp.int32),
            pltpu.VMEM((48, 128), F32),
            pltpu.VMEM((9, 48, 128), BF16),
            pltpu.VMEM((96, 128), F32),
            pltpu.VMEM((9 * HOME + 1, 8, 128), F32),
            pltpu.VMEM((96, 128), F32),
            pltpu.VMEM((2, 24, 128), F32),
            pltpu.VMEM((ROWS, WIN), BF16),
            pltpu.VMEM((128, 128), F32),
            pltpu.VMEM((WIN, 1024), BF16),
            pltpu.VMEM((256, 256), BF16),
            pltpu.VMEM((256, 256), BF16),
            pltpu.VMEM((128, 1024), BF16),
            big,
            big,
            big,
            big,
            big,
            big,
            pltpu.VMEM((ROWS, 128), BF16),
            pltpu.VMEM((96, 128), F32),
            pltpu.VMEM((384, 128), F32),
            pltpu.VMEM((384, 128), F32),
            pltpu.VMEM((3, 8, 128), F32),
            pltpu.VMEM((8, 3, 8, 128), F32),
            pltpu.VMEM((4, 8, 128), jnp.int32),
            tiles,
            tiles,
            pltpu.VMEM((192, 128), F32),
            pltpu.VMEM((192, 128), F32),
            piece,
            piece,
            piece,
            dma(8),
            dma(8),
            dma(8),
            dma(8),
            dma(8),
            dma(4),
            dma(4),
            dma(4),
            dma(4),
            dma(2),
            dma(2),
            dma(16),
            dma(16),
            dma(16),
            dma(16),
            dma(16),
            dma(16),
        ],
        compiler_params=pltpu.CompilerParams(
            collective_id=0, has_side_effects=True, vmem_limit_bytes=63 << 20
        ),
        name="train",
    )(vof, target, neighbours, live_blocks, pick, w_first, w_mid, w_last)


def shards(vof, target, neighbours, live_blocks, pick, w_first, w_mid, w_last):
    sums, tiles = train(
        vof,
        target,
        neighbours,
        live_blocks,
        pick,
        w_first,
        w_mid,
        w_last.reshape(1, 128),
    )
    pred, gfirst, gmid, glast = pl.pallas_call(
        write_kernel,
        out_shape=(
            jax.ShapeDtypeStruct((8, 512), F32),
            jax.ShapeDtypeStruct((125, 128), F32),
            jax.ShapeDtypeStruct((2, 128, 128), F32),
            jax.ShapeDtypeStruct((1, 128), F32),
        ),
        in_specs=[VMEM, VMEM],
        out_specs=(VMEM, VMEM, VMEM, VMEM),
        scratch_shapes=[pltpu.VMEM((384, 128), F32)],
        name="write",
    )(sums, tiles)
    return pred, gfirst, gmid, glast.reshape(128)


def solution(mesh):
    both = ("stream", "cross")
    return jax.shard_map(
        shards,
        mesh=mesh,
        in_specs=(
            P(both, None),
            P(both, None),
            P(both, None),
            P(both),
            P(both, None),
            P(),
            P(),
            P(),
        ),
        out_specs=(P(both, None), P(), P(), P()),
        check_vma=False,
    )
```

time: 78.8 us -> 66.4 us (0.84)
  local copies, waits for them, and re-layouts: 6.7 us -> 0 us
  Pallas kernels: 70.3 us -> 65 us
    unnamed x18 -> x0, local copies, waits for them, and re-layouts: 6.7 us -> none
    pallas_call x3 -> x2, Pallas kernels: 70.3 us -> 65 us  [the longest x1 63.3 us: train(): pl.pallas_call(train_kernel, out_shape=(jax.ShapeDtypeStruct((2, 16, PIEC...]
where the time goes in v2:
time: 66.4 us; the launch traced here: 66.3 us
  Pallas kernels  65 us (98%)
  between operations  1.29 us (2%)
    pallas_call x1, Pallas kernels, train(): pl.pallas_call(train_kernel, out_shape=(jax.ShapeDtypeStruct((2, 16, PIEC...  63.3 us
    pallas_call x1, Pallas kernels, shards(): pl.pallas_call(write_kernel, out_shape=(jax.ShapeDtypeStruct((8, 512), F3...  1.7 us

profile of v2, /device:TPU:1, one launch (start us, length us, event | category | flops | bytes accessed | tf_op | source)
XLA Modules:
  0.0 66.3 jit_solution(1127277618682164541)
XLA Ops:
  1.3 63.3 %train.1 = (f32[2,16,12,128]{3,2,1,0:T(8,128)}, f32[64,128]{1,0:T(8,128)}) custom-call(bf16[12,512]{1,0:T(8,128)(2,1)} %vof_hbm.1, bf16[12,512]{1,0:T(8,128)(2,1)} %target_hbm.1, s32[12,26]{1,0:T(8,128)} %nbr_hbm.1, s32[1]{0:T(128)S(6)} %copy.12.live_hbm, s32[1,2]{1,0:T(1,128)} %pick_hbm.1, bf16[125,128]{1,0:T(8,128)(2,1)} %w1_hbm.1, ...), custom_call_target="tpu_custom_call" | custom-call | tf_op jit(solution)/shard_map/train/pallas_call | solution.py:584
  64.6 1.7 %write.1 = (f32[8,512]{1,0:T(8,128)}, f32[125,128]{1,0:T(8,128)}, f32[2,128,128]{2,1,0:T(8,128)}, f32[1,128]{1,0:T(1,128)}) custom-call(f32[2,16,12,128]{3,2,1,0:T(8,128)} %get-tuple-element.10.sum_ref, f32[64,128]{1,0:T(8,128)} %get-tuple-element.11.tile_ref), custom_call_target="tpu_custom_call" | custom-call | tf_op jit(solution)/shard_map/write/pallas_call | solution.py:671

commit v3 on v2

--- a/solution.py
+++ b/solution.py
@@ -106,10 +106,10 @@
             )
         low = jnp.where(lane < 24, shift(row[0], -72), shift(row[1], 24))
         high = jnp.where(lane < 72, shift(row[1], -24), shift(row[2], 72))
-        pad[0, 8 * dy : 8 * dy + 8, :] = low
-        pad[1, 8 * dy : 8 * dy + 8, :] = high
+        pad[2 * b, 8 * dy : 8 * dy + 8, :] = low
+        pad[2 * b + 1, 8 * dy : 8 * dy + 8, :] = high
     for half in range(2):
-        a = [pad[half, 6 + ay : 14 + ay, :] for ay in range(5)]
+        a = [pad[2 * b + half, 6 + ay : 14 + ay, :] for ay in range(5)]
         odd = [shift(a[1], 64), shift(a[3], 64)]
         made = []
         for x in range(4):
@@ -124,13 +124,12 @@
         for pair in range(2):
             for g in range(3):
                 both = jnp.concatenate([made[2 * pair][g], made[2 * pair + 1][g]], axis=0)
-                base = pl.multiple_of(64 * b, 64) + 32 * half + 16 * pair
-                xs[pl.ds(pl.multiple_of(base, 16), 16), 128 * g : 128 * g + 128] = both.astype(BF16)
+                base = 64 * b + 32 * half + 16 * pair
+                xs[base : base + 16, 128 * g : 128 * g + 128] = both.astype(BF16)
 
 
 STEPS = [(a, b) for a in (-1, 0, 1) for b in (-1, 0, 1) if (a, b) != (0, 0)]
 STEPS.sort(key=lambda step: (step[1] == 0, step[0] == 0))
-CHUNK = 256
 
 
 def train_kernel(
@@ -380,68 +379,58 @@
 
     to_scalar.wait()
 
-    @pl.loop(0, HOME)
-    def _(b):
+    for b in range(HOME):
         build_window(b, lookup_ref, tab, pad, xs)
 
     live = jnp.full((8, 128), live_ref[0], jnp.int32)
 
-    def train(c):
-        at = pl.ds(pl.multiple_of(c * CHUNK, CHUNK), CHUNK)
-        window = xs[at, :]
-        predicted = jnp.zeros((CHUNK, 128), F32)
-        for j in range(4):
-            col = slice(256 * j, 256 * j + 256)
-            a = jnp.tanh(dot(window, t[:, col])).astype(BF16)
-            h1[at, col] = a
-            a = jnp.tanh(dot(a, bd2[...])).astype(BF16)
-            h2[at, col] = a
-            a = jnp.tanh(dot(a, bd3[...])).astype(BF16)
-            h3[at, col] = a
-            predicted += dot_n(a, wle[:, col])
-        for i in range(CHUNK // 64):
-            b = c * (CHUNK // 64) + i
-            tile = jnp.zeros((8, 128), F32)
-            for k in range(8):
-                part = predicted[64 * i + 8 * k : 64 * i + 8 * k + 8]
-                tile = jnp.where(((lane >> 3) & 7) == k, part, tile)
-            rows = pl.ds(pl.multiple_of(b * 8, 8), 8)
-            mask = jnp.where(b < live, 1.0, 0.0).astype(F32)
-            pt[rows, :] = tile
-            res = ((tile * mask - tt[rows, :]) * mask / SCALE).astype(BF16).astype(F32)
-            for k in range(4):
-                both = jnp.concatenate(
-                    [
-                        jnp.where((lane >> 3) == 2 * k, res, 0.0),
-                        jnp.where((lane >> 3) == 2 * k + 1, res, 0.0),
-                    ],
-                    axis=0,
-                )
-                r2[pl.ds(pl.multiple_of(b * 64 + 16 * k, 16), 16), :] = both.astype(BF16)
-        rr = r2[at, :]
-        for j in range(4):
-            col = slice(256 * j, 256 * j + 256)
-            h = h3[at, col].astype(F32)
-            d = (dot(rr, wle[:, col]) * (1.0 - h * h)).astype(BF16)
-            d3[at, col] = d
-            h = h2[at, col].astype(F32)
-            d = (dot_n(d, bd3[...]) * (1.0 - h * h)).astype(BF16)
-            d2[at, col] = d
-            h = h1[at, col].astype(F32)
-            d = (dot_n(d, bd2[...]) * (1.0 - h * h)).astype(BF16)
-            d1[at, col] = d
-
-    @pl.loop(0, 3)
-    def _(c):
-        train(2 - c)
-
-        @pl.when(c == 1)
-        def _():
-            for i in range(3):
-                at = 8 * (KEEP + 2 * i)
-                extra[i] = jnp.where(lane < 64, pt[at : at + 8, :], pt[at + 8 : at + 16, :])
-            eb[xc] = extra[...]
-            start(8, xc, row_copy)
+    window = xs[...]
+    predicted = jnp.zeros((ROWS, 128), F32)
+    for j in range(4):
+        col = slice(256 * j, 256 * j + 256)
+        a = jnp.tanh(dot(window, t[:, col])).astype(BF16)
+        h1[:, col] = a
+        a = jnp.tanh(dot(a, bd2[...])).astype(BF16)
+        h2[:, col] = a
+        a = jnp.tanh(dot(a, bd3[...])).astype(BF16)
+        h3[:, col] = a
+        predicted += dot_n(a, wle[:, col])
+    for b in range(HOME):
+        tile = jnp.zeros((8, 128), F32)
+        for k in range(8):
+            part = predicted[64 * b + 8 * k : 64 * b + 8 * k + 8]
+            tile = jnp.where(((lane >> 3) & 7) == k, part, tile)
+        pt[8 * b : 8 * b + 8, :] = tile
+    for i in range(3):
+        at = 8 * (KEEP + 2 * i)
+        extra[i] = jnp.where(lane < 64, pt[at : at + 8, :], pt[at + 8 : at + 16, :])
+    eb[xc] = extra[...]
+    start(8, xc, row_copy)
+    for b in range(HOME):
+        rows = slice(8 * b, 8 * b + 8)
+        mask = jnp.where(b < live, 1.0, 0.0).astype(F32)
+        res = ((pt[rows, :] * mask - tt[rows, :]) * mask / SCALE).astype(BF16).astype(F32)
+        for k in range(4):
+            both = jnp.concatenate(
+                [
+                    jnp.where((lane >> 3) == 2 * k, res, 0.0),
+                    jnp.where((lane >> 3) == 2 * k + 1, res, 0.0),
+                ],
+                axis=0,
+            )
+            r2[64 * b + 16 * k : 64 * b + 16 * k + 16, :] = both.astype(BF16)
+    rr = r2[...]
+    for j in range(4):
+        col = slice(256 * j, 256 * j + 256)
+        h = h3[:, col].astype(F32)
+        d = (dot(rr, wle[:, col]) * (1.0 - h * h)).astype(BF16)
+        d3[:, col] = d
+        h = h2[:, col].astype(F32)
+        d = (dot_n(d, bd3[...]) * (1.0 - h * h)).astype(BF16)
+        d2[:, col] = d
+        h = h1[:, col].astype(F32)
+        d = (dot_n(d, bd2[...]) * (1.0 - h * h)).astype(BF16)
+        d1[:, col] = d
 
     second = jnp.zeros((128, 128), F32)
     third = jnp.zeros((128, 128), F32)
@@ -605,7 +594,7 @@
             pltpu.VMEM((96, 128), F32),
             pltpu.VMEM((9 * HOME + 1, 8, 128), F32),
             pltpu.VMEM((96, 128), F32),
-            pltpu.VMEM((2, 24, 128), F32),
+            pltpu.VMEM((2 * HOME, 24, 128), F32),
             pltpu.VMEM((ROWS, WIN), BF16),
             pltpu.VMEM((128, 128), F32),
             pltpu.VMEM((WIN, 1024), BF16),

time: 66.4 us -> 60.1 us (0.905)
  Pallas kernels: 65 us -> 58.7 us
    pallas_call x1, Pallas kernels: 63.3 us -> 57 us  [train(): pl.pallas_call(train_kernel, out_shape=(jax.ShapeDtypeStruct((2, 16, PIEC...]
where the time goes in v3:
time: 60.1 us; the launch traced here: 60 us
  Pallas kernels  58.7 us (98%)
  between operations  1.29 us (2%)
    pallas_call x1, Pallas kernels, train(): pl.pallas_call(train_kernel, out_shape=(jax.ShapeDtypeStruct((2, 16, PIEC...  57 us
    pallas_call x1, Pallas kernels, shards(): pl.pallas_call(write_kernel, out_shape=(jax.ShapeDtypeStruct((8, 512), F3...  1.7 us

profile of v3, /device:TPU:1, one launch (start us, length us, event | category | flops | bytes accessed | tf_op | source)
XLA Modules:
  0.0 60.0 jit_solution(11596048378955974948)
XLA Ops:
  1.3 57.0 %train.1 = (f32[2,16,12,128]{3,2,1,0:T(8,128)}, f32[64,128]{1,0:T(8,128)}) custom-call(bf16[12,512]{1,0:T(8,128)(2,1)} %vof_hbm.1, bf16[12,512]{1,0:T(8,128)(2,1)} %target_hbm.1, s32[12,26]{1,0:T(8,128)} %nbr_hbm.1, s32[1]{0:T(128)S(6)} %copy.12.live_hbm, s32[1,2]{1,0:T(1,128)} %pick_hbm.1, bf16[125,128]{1,0:T(8,128)(2,1)} %w1_hbm.1, ...), custom_call_target="tpu_custom_call" | custom-call | tf_op jit(solution)/shard_map/train/pallas_call | solution.py:573
  58.3 1.7 %write.1 = (f32[8,512]{1,0:T(8,128)}, f32[125,128]{1,0:T(8,128)}, f32[2,128,128]{2,1,0:T(8,128)}, f32[1,128]{1,0:T(1,128)}) custom-call(f32[2,16,12,128]{3,2,1,0:T(8,128)} %get-tuple-element.10.sum_ref, f32[64,128]{1,0:T(8,128)} %get-tuple-element.11.tile_ref), custom_call_target="tpu_custom_call" | custom-call | tf_op jit(solution)/shard_map/write/pallas_call | solution.py:660

commit v4 on v3

--- a/solution.py
+++ b/solution.py
@@ -155,7 +155,6 @@
     lookup_ref,
     packed,
     table,
-    tall,
     tab,
     tt,
     pad,
@@ -276,8 +275,8 @@
     fetches[0].wait()
     rows = vof_ref[...].astype(F32)
     for i in range(4):
-        packed[HOME * i : HOME * i + HOME, :] = rows[:, 128 * i : 128 * i + 128]
-    table[4] = packed[...].astype(BF16)
+        packed[4, HOME * i : HOME * i + HOME, :] = rows[:, 128 * i : 128 * i + 128]
+    table[4] = packed[4].astype(BF16)
 
     pl.semaphore_wait(barrier, count)
 
@@ -362,20 +361,25 @@
     tab[9 * HOME] = jnp.zeros((8, 128), F32)
 
     def unpack(slot):
-        packed[...] = table[slot].astype(F32)
-        parts = [packed[HOME * i : HOME * i + HOME, :] for i in range(4)]
-        spread(parts, keep_in(tall), 12, 2)
-        for i in range(HOME):
-            tab[HOME * slot + i] = tall[8 * i : 8 * i + 8, :]
-
-    unpack(4)
-    for k in reversed(range(8)):
-
+        packed[slot] = table[slot].astype(F32)
+        parts = [packed[slot, HOME * i : HOME * i + HOME, :] for i in range(4)]
+
+        def keep(y, tile):
+            tab[HOME * slot : HOME * slot + HOME, y, :] = tile
+
+        spread(parts, keep, 12, 2)
+
+    def await_halo(k):
         @pl.when(near[k][0])
         def _():
             halo_copy(k, slot_of(*STEPS[k]), k).wait_recv()
 
-        unpack(slot_of(*STEPS[k]))
+    unpack(4)
+    for group in (range(6, 8), range(6)):
+        for k in group:
+            await_halo(k)
+        for k in group:
+            unpack(slot_of(*STEPS[k]))
 
     to_scalar.wait()
 
@@ -441,27 +445,6 @@
     flat[0:128, :] = second
     flat[128:256, :] = third
 
-    arrive(4, zhi, pick_copy)
-    arrive(8, xc, row_copy)
-    ob[...] = jnp.zeros_like(ob)
-    wants = [pk[q] for q in range(4)]
-
-    @pl.loop(0, 8)
-    def _(d):
-        for i in range(3):
-            tile = eb[d, i]
-            swapped = shift(tile, 64)
-            name = (zhi * 8 + d) * KEEP + 2 * i
-            first = jnp.where(lane < 64, tile, swapped)
-            other = jnp.where(lane < 64, swapped, tile)
-            for q in range(4):
-                old = ob[q]
-                old = jnp.where(wants[q] == name, first, old)
-                ob[q] = jnp.where(wants[q] == name + 1, other, old)
-
-    start(4, zhi, out_copy)
-    rb[zhi] = ob[zhi]
-
     total = jnp.zeros((WIN, 128), F32)
     xv = xs[...]
     for j in range(4):
@@ -497,6 +480,28 @@
         hs[i] = half[PIECE * i : PIECE * i + PIECE, :]
     start(16, xy, xy_copy)
     rs[xy] = hs[xy]
+
+    arrive(4, zhi, pick_copy)
+    arrive(8, xc, row_copy)
+    ob[...] = jnp.zeros_like(ob)
+    wants = [pk[q] for q in range(4)]
+
+    @pl.loop(0, 8)
+    def _(d):
+        for i in range(3):
+            tile = eb[d, i]
+            swapped = shift(tile, 64)
+            name = (zhi * 8 + d) * KEEP + 2 * i
+            first = jnp.where(lane < 64, tile, swapped)
+            other = jnp.where(lane < 64, swapped, tile)
+            for q in range(4):
+                old = ob[q]
+                old = jnp.where(wants[q] == name, first, old)
+                ob[q] = jnp.where(wants[q] == name + 1, other, old)
+
+    start(4, zhi, out_copy)
+    rb[zhi] = ob[zhi]
+
     arrive(16, xy, xy_copy)
     total = rs[0]
     for i in range(1, 16):
@@ -530,10 +535,10 @@
         total += zb[i]
     sum_ref[core, xy] = total
     start(16, xy, all_copy)
-    sent(16, zz, z_copy)
     arrive(16, xy, all_copy)
     last_pair = remote(sum_ref.at[core], sum_ref.at[core], cs_s.at[1], cs_r.at[1], pair)
     last_pair.start()
+    sent(16, zz, z_copy)
     sent(16, xy, all_copy)
     last_pair.wait_send()
     remote(
@@ -589,9 +594,8 @@
             pltpu.VMEM((1, 128), BF16),
             pltpu.VMEM((HOME, 26), jnp.int32),
             pltpu.SMEM((HOME, 26), jnp.int32),
-            pltpu.VMEM((48, 128), F32),
+            pltpu.VMEM((9, 48, 128), F32),
             pltpu.VMEM((9, 48, 128), BF16),
-            pltpu.VMEM((96, 128), F32),
             pltpu.VMEM((9 * HOME + 1, 8, 128), F32),
             pltpu.VMEM((96, 128), F32),
             pltpu.VMEM((2 * HOME, 24, 128), F32),

time: 60.1 us -> 58.2 us (0.968)
  Pallas kernels: 58.7 us -> 56.8 us
    pallas_call x1, Pallas kernels: 57 us -> 55.1 us  [train(): pl.pallas_call(train_kernel, out_shape=(jax.ShapeDtypeStruct((2, 16, PIEC...]
where the time goes in v4:
time: 58.2 us; the launch traced here: 58.1 us
  Pallas kernels  56.8 us (98%)
  between operations  1.29 us (2%)
    pallas_call x1, Pallas kernels, train(): pl.pallas_call(train_kernel, out_shape=(jax.ShapeDtypeStruct((2, 16, PIEC...  55.1 us
    pallas_call x1, Pallas kernels, shards(): pl.pallas_call(write_kernel, out_shape=(jax.ShapeDtypeStruct((8, 512), F3...  1.7 us

profile of v4, /device:TPU:1, one launch (start us, length us, event | category | flops | bytes accessed | tf_op | source)
XLA Modules:
  0.0 58.1 jit_solution(9807171243953646134)
XLA Ops:
  1.3 55.1 %train.1 = (f32[2,16,12,128]{3,2,1,0:T(8,128)}, f32[64,128]{1,0:T(8,128)}) custom-call(bf16[12,512]{1,0:T(8,128)(2,1)} %vof_hbm.1, bf16[12,512]{1,0:T(8,128)(2,1)} %target_hbm.1, s32[12,26]{1,0:T(8,128)} %nbr_hbm.1, s32[1]{0:T(128)S(6)} %copy.12.live_hbm, s32[1,2]{1,0:T(1,128)} %pick_hbm.1, bf16[125,128]{1,0:T(8,128)(2,1)} %w1_hbm.1, ...), custom_call_target="tpu_custom_call" | custom-call | tf_op jit(solution)/shard_map/train/pallas_call | solution.py:578
  56.4 1.7 %write.1 = (f32[8,512]{1,0:T(8,128)}, f32[125,128]{1,0:T(8,128)}, f32[2,128,128]{2,1,0:T(8,128)}, f32[1,128]{1,0:T(1,128)}) custom-call(f32[2,16,12,128]{3,2,1,0:T(8,128)} %get-tuple-element.10.sum_ref, f32[64,128]{1,0:T(8,128)} %get-tuple-element.11.tile_ref), custom_call_target="tpu_custom_call" | custom-call | tf_op jit(solution)/shard_map/write/pallas_call | solution.py:664

commit v5 on v4

--- a/solution.py
+++ b/solution.py
@@ -436,12 +436,14 @@
         d = (dot_n(d, bd2[...]) * (1.0 - h * h)).astype(BF16)
         d1[:, col] = d
 
-    second = jnp.zeros((128, 128), F32)
-    third = jnp.zeros((128, 128), F32)
-    for z in range(8):
-        col = slice(128 * z, 128 * z + 128)
+    second = jnp.zeros((256, 256), F32)
+    third = jnp.zeros((256, 256), F32)
+    for j in range(4):
+        col = slice(256 * j, 256 * j + 256)
         second += dot_t(h1[:, col], d2[:, col])
         third += dot_t(h2[:, col], d3[:, col])
+    second = second[0:128, 0:128] + second[128:256, 128:256]
+    third = third[0:128, 0:128] + third[128:256, 128:256]
     flat[0:128, :] = second
     flat[128:256, :] = third
 

time: 58.2 us -> 57.9 us (level)
  no operation moved by 1% of the time
where the time goes in v5:
time: 57.9 us; the launch traced here: 57.7 us
  Pallas kernels  56.4 us (97%)
  between operations  1.29 us (2%)
    pallas_call x1, Pallas kernels, train(): pl.pallas_call(train_kernel, out_shape=(jax.ShapeDtypeStruct((2, 16, PIEC...  54.7 us
    pallas_call x1, Pallas kernels, shards(): pl.pallas_call(write_kernel, out_shape=(jax.ShapeDtypeStruct((8, 512), F3...  1.7 us

profile of v5, /device:TPU:1, one launch (start us, length us, event | category | flops | bytes accessed | tf_op | source)
XLA Modules:
  0.0 57.7 jit_solution(12047698412659131435)
XLA Ops:
  1.3 54.7 %train.1 = (f32[2,16,12,128]{3,2,1,0:T(8,128)}, f32[64,128]{1,0:T(8,128)}) custom-call(bf16[12,512]{1,0:T(8,128)(2,1)} %vof_hbm.1, bf16[12,512]{1,0:T(8,128)(2,1)} %target_hbm.1, s32[12,26]{1,0:T(8,128)} %nbr_hbm.1, s32[1]{0:T(128)S(6)} %copy.12.live_hbm, s32[1,2]{1,0:T(1,128)} %pick_hbm.1, bf16[125,128]{1,0:T(8,128)(2,1)} %w1_hbm.1, ...), custom_call_target="tpu_custom_call" | custom-call | tf_op jit(solution)/shard_map/train/pallas_call | solution.py:580
  56.0 1.7 %write.1 = (f32[8,512]{1,0:T(8,128)}, f32[125,128]{1,0:T(8,128)}, f32[2,128,128]{2,1,0:T(8,128)}, f32[1,128]{1,0:T(1,128)}) custom-call(f32[2,16,12,128]{3,2,1,0:T(8,128)} %get-tuple-element.10.sum_ref, f32[64,128]{1,0:T(8,128)} %get-tuple-element.11.tile_ref), custom_call_target="tpu_custom_call" | custom-call | tf_op jit(solution)/shard_map/write/pallas_call | solution.py:666
